TPU v7x, 32 devices: a whole 2x2x4 slice. The times are simulated.
32 devices in a mesh: dp: 8 (over z, x), mp: 4 (over y, core).
Axes of the slice: x: 2, y: 2, z: 4, core: 2. Of those that a mesh axis runs over, the one named last changes fastest.
Arguments:
- teacher_query: bfloat16 [512, 8192], P('mp', 'dp'), may hold values from -120 to 120
- teacher_keys: bfloat16 [512, 1024], P('mp'), may hold values from -6 to 6
- teacher_values: bfloat16 [512, 1024], P('mp'), may hold values from -6 to 6
- teacher_out: bfloat16 [8192, 8192], P('dp', 'mp'), may hold values from -0.0625 to 0.0625
- teacher_resid: bfloat16 [512, 8192], P('dp', 'mp'), may hold values from -1.5 to 1.5
- distill_proj: bfloat16 [8192, 4096], P('mp', 'dp'), may hold values from -1 to 2
- student_context: bfloat16 [512, 4096], P('mp'), may hold values from -6 to 6
- student_resid: bfloat16 [512, 4096], P('mp', 'dp'), may hold values from -3 to 3
- student_out: bfloat16 [4096, 4096], P(None, 'dp'), may hold values from -0.09375 to 0.09375
- student_gain: float32 [4096], replicated, may hold values from 0.5 to 1.5
Outputs:
- grad_wo: bfloat16 [4096, 4096], P(None, 'dp')
- grad_gain: float32 [4096], P('dp')
- grad_proj: float32 [8192, 4096], P('mp', 'dp')
All inputs are finite; a program needn't handle non-finite values.
Results may differ from a plain program's by a relative error of at most 0.03.
Values may be sent and summed in bfloat16 or wider, within the bound.
A program may use at most 64 MiB of HBM per device.

v0:
```python
import jax
import jax.numpy as jnp
from jax import lax
from jax.sharding import PartitionSpec as P

HEADS = 64
KV_HEADS = 8
HEAD = 128


EPS = 1e-05


def on_device(
    teacher_query,
    teacher_keys,
    teacher_values,
    teacher_out,
    teacher_resid,
    distill_proj,
    student_context,
    student_resid,
    student_out,
    student_gain,
):
    groups = HEADS // KV_HEADS
    dp_index = lax.axis_index("dp")
    mp_index = lax.axis_index("mp")
    query_rows, query_width = teacher_query.shape
    local_heads = query_width // HEAD
    kv_local = max(local_heads // groups, 1)
    kv_start = dp_index * local_heads // groups
    key_mine = lax.dynamic_slice_in_dim(teacher_keys, kv_start * HEAD, kv_local * HEAD, 1)
    value_mine = lax.dynamic_slice_in_dim(teacher_values, kv_start * HEAD, kv_local * HEAD, 1)
    keys_all, values_all = (
        lax.all_gather(key_mine, "mp", axis=0, tiled=True),
        lax.all_gather(value_mine, "mp", axis=0, tiled=True),
    )
    total = keys_all.shape[0]
    repeat = local_heads // kv_local
    queries = teacher_query.reshape(query_rows, kv_local, repeat, HEAD)
    keyed = keys_all.reshape(total, kv_local, HEAD)
    valued = values_all.reshape(total, kv_local, HEAD)
    scores = jnp.einsum(
        "qgrd,kgd->grqk", queries, keyed, preferred_element_type=jnp.float32
    ) * HEAD ** (-0.5)
    query_pos = mp_index * query_rows + lax.iota(jnp.int32, query_rows)
    key_pos = lax.iota(jnp.int32, total)
    allowed = query_pos[:, None] >= key_pos[None, :]
    scores = jnp.where(allowed, scores, -jnp.inf)
    top = jnp.max(scores, axis=-1, keepdims=True)
    weights = jnp.exp(scores - top)
    probs = (weights / jnp.sum(weights, axis=-1, keepdims=True)).astype(jnp.bfloat16)
    context = jnp.einsum("grqk,kgd->qgrd", probs, valued, preferred_element_type=jnp.float32)
    context = context.astype(jnp.bfloat16).reshape(query_rows, query_width)
    head_terms = jnp.dot(
        lax.all_gather(context, "mp", axis=0, tiled=True),
        teacher_out,
        preferred_element_type=jnp.float32,
    )
    summed = lax.psum_scatter(
        head_terms.astype(jnp.bfloat16), "dp", scatter_dimension=0, tiled=True
    ).astype(jnp.float32)
    hidden = (teacher_resid.astype(jnp.float32) + summed).astype(jnp.bfloat16)
    hidden_all = lax.all_gather(hidden, "dp", axis=0, tiled=True)
    rows = hidden_all
    target = lax.psum_scatter(
        jnp.dot(rows, distill_proj, preferred_element_type=jnp.float32),
        "mp",
        scatter_dimension=0,
        tiled=True,
    )
    width = student_context.shape[1]
    columns = student_out.shape[1]
    state = student_resid.astype(jnp.float32) + jnp.dot(
        student_context, student_out, preferred_element_type=jnp.float32
    )
    grad_scale = total ** (-0.5)
    gain_mine = lax.dynamic_slice_in_dim(student_gain, dp_index * columns, columns, 0)
    squares = lax.psum(jnp.sum(state * state, axis=1), "dp")
    inverse = lax.rsqrt(squares / width + EPS)[:, None]
    pred = state * inverse * gain_mine
    error = (pred - target) * grad_scale
    upstream = error * gain_mine
    inner = lax.psum(jnp.sum(upstream * state, axis=1), "dp")
    grad_state = inverse * upstream - state * inverse**3 * (inner / width)[:, None]
    gain_term = error * state * inverse
    grad_bf = grad_state.astype(jnp.bfloat16)
    error_bf = error.astype(jnp.bfloat16)
    gain_part = jnp.sum(gain_term, axis=0)
    contract_rows = (((0,), (0,)), ((), ()))
    weight_part = lax.dot_general(
        student_context, grad_bf, contract_rows, preferred_element_type=jnp.float32
    )
    weight_sum, gain_sum = lax.psum((weight_part, gain_part), "mp")
    grad_wo = weight_sum.astype(jnp.bfloat16)
    empty = jnp.zeros((hidden_all.shape[1], columns), jnp.float32)
    rows = hidden_all
    grad_proj = empty - lax.dot_general(
        rows,
        lax.all_gather(error_bf, "mp", axis=0, tiled=True),
        contract_rows,
        preferred_element_type=jnp.float32,
    )
    return (grad_wo, gain_sum, grad_proj)


def solution(mesh):
    in_specs = (
        P("mp", "dp"),
        P("mp", None),
        P("mp", None),
        P("dp", "mp"),
        P("dp", "mp"),
        P("mp", "dp"),
        P("mp", None),
        P("mp", "dp"),
        P(None, "dp"),
        P(),
    )
    out_specs = (P(None, "dp"), P("dp"), P("mp", "dp"))
    return jax.shard_map(
        on_device, mesh=mesh, in_specs=in_specs, out_specs=out_specs, check_vma=False
    )
```

profile of v0, /device:TPU:0, one launch (start us, length us, event | category | flops | bytes accessed | tf_op | source)
XLA Modules:
  0.0 397.8 jit_solution(6231478412914924942)
XLA Ops:
  7.2 0.9 constant_dynamic-slice_fusion
  8.1 6.5 %all_gather.16 = bf16[512,128]{1,0:T(8,128)(2,1)S(1)} all-gather(bf16[128,128]{1,0:T(8,128)(2,1)S(1)} %constant_dynamic-slice_fusion), channel_id=1, replica_groups=mesh['dp'=8,'mp'=4] {'mp'}, dimensions={0}, use_global_device_ids=true | all-gather | bytes 163840 | tf_op jit(solution)/shard_map/all_gather | solution.py:36
  14.7 0.8 constant_dynamic-slice_fusion.1
  15.6 5.6 %all_gather.15 = bf16[512,128]{0,1:T(8,128)(2,1)S(1)} all-gather(bf16[128,128]{0,1:T(8,128)(2,1)S(1)} %copy.18), channel_id=1, replica_groups=mesh['dp'=8,'mp'=4] {'mp'}, dimensions={0}, use_global_device_ids=true | all-gather | bytes 163840 | tf_op jit(solution)/shard_map/all_gather | solution.py:37
  21.2 1.4 fusion.10
  22.9 1.2 convolution_convert_fusion.1
  24.2 18.4 %all-gather.3.cloned.1.call-done = bf16[512,1024]{0,1:T(8,128)(2,1)} async-done(((bf16[128,1024]{0,1:T(8,128)(2,1)}), bf16[512,1024]{0,1:T(8,128)(2,1)}) %all-gather.3.cloned.1.call-update) | async-done | bytes 1048592 | tf_op jit(solution)/shard_map/all_gather | solution.py:57
  42.6 6.2 %convolution_convert_fusion = bf16[512,2048]{1,0:T(8,128)(2,1)} fusion(bf16[512,1024]{0,1:T(8,128)(2,1)} %all-gather.3.cloned.1.call-done, bf16[1024,2048]{1,0:T(8,128)(2,1)} %param.13), kind=kOutput, calls=%fused_computation.2 | convolution fusion | flops 2148532224 | bytes 7340032 | tf_op jit(solution)/shard_map/dot_general | solution.py:56
  48.9 68.4 %reduce-scatter.3.cloned.1.call-done = bf16[64,2048]{1,0:T(8,128)(2,1)} async-done(((bf16[512,2048]{1,0:T(8,128)(2,1)}), bf16[64,2048]{1,0:T(8,128)(2,1)}) %reduce-scatter.3.cloned.1.call-update) | async-done | bytes 262160 | tf_op jit(solution)/shard_map/reduce_scatter | solution.py:61
  117.3 1.7 add_convert_fusion
  119.1 49.2 %all-gather.5.cloned.1.call-done = bf16[512,2048]{1,0:T(8,128)(2,1)} async-done(((bf16[64,2048]{1,0:T(8,128)(2,1)}), bf16[512,2048]{1,0:T(8,128)(2,1)}) %all-gather.5.cloned.1.call-update) | async-done | bytes 2097168 | tf_op jit(solution)/shard_map/all_gather | solution.py:65
  168.3 3.8 fusion.11
  172.2 3.0 multiply_reduce_fusion.2
  175.2 18.9 %psum.28 = f32[128]{0:T(128)S(1)} all-reduce(f32[128]{0:T(128)S(1)} %get-tuple-element.15), channel_id=1, replica_groups=mesh['dp'=8,'mp'=4] {'dp'}, use_global_device_ids=true, to_apply=%region_1.2 | all-reduce | flops 128 | bytes 1024 | tf_op jit(solution)/shard_map/psum | solution.py:80
  194.1 0.8 broadcast_multiply_fusion
  194.9 0.5 multiply_multiply_fusion
  195.7 1.7 multiply_reduce_fusion
  197.4 22.0 %psum.29 = f32[128]{0:T(128)} all-reduce(f32[128]{0:T(128)} %get-tuple-element.7), channel_id=1, replica_groups=mesh['dp'=8,'mp'=4] {'dp'}, use_global_device_ids=true, to_apply=%region_7.8 | all-reduce | flops 128 | bytes 1024 | tf_op jit(solution)/shard_map/psum | solution.py:85
  219.4 0.7 broadcast_multiply_fusion.1
  220.0 5.6 %convolution_bitcast_fusion = f32[4096,512]{0,1:T(8,128)} fusion(bf16[128,4096]{1,0:T(8,128)(2,1)S(1)} %copy-done.1, f32[128,512]{1,0:T(8,128)S(1)} %get-tuple-element.16, f32[128]{0:T(128)S(1)} %broadcast_multiply_fusion.1, f32[128]{0:T(128)} %get-tuple-element.13, f32[512]{0:T(512)S(1)} %get-tuple-element.10, f32[128]{0:T(128)S(1)} %get-tuple-element.14, ...), kind=kOutput, calls=%fused_computation | convolution fusion | flops 537460736 | bytes 9967104 | tf_op jit(solution)/shard_map/dot_general | solution.py:92
  225.6 147.1 %all-reduce.2 = (bf16[4096,512]{0,1:T(8,128)(2,1)}, f32[512]{0:T(512)}) all-reduce(f32[4096,512]{0,1:T(8,128)} %convolution_bitcast_fusion, f32[512]{0:T(512)S(1)} %get-tuple-element.6), channel_id=1, replica_groups=mesh['dp'=8,'mp'=4] {'mp'}, use_global_device_ids=true, to_apply=%region_8.9 | all-reduce | flops 2097664 | bytes 12587008 | tf_op jit(solution)/shard_map/psum | solution.py:95
  372.7 6.4 %copy.16 = bf16[4096,512]{1,0:T(8,128)(2,1)} copy(bf16[4096,512]{0,1:T(8,128)(2,1)} %get-tuple-element.8) | data formatting | bytes 8388608
  379.1 7.3 %all_gather.19 = bf16[512,512]{1,0:T(8,128)(2,1)S(1)} all-gather(bf16[128,512]{1,0:T(8,128)(2,1)S(1)} %get-tuple-element.12), channel_id=1, replica_groups=mesh['dp'=8,'mp'=4] {'mp'}, dimensions={0}, use_global_device_ids=true | all-gather | bytes 655360 | tf_op jit(solution)/shard_map/all_gather | solution.py:101
  386.4 4.9 %convolution_subtract_fusion = f32[2048,512]{1,0:T(8,128)} fusion(bf16[512,2048]{1,0:T(8,128)(2,1)} %all-gather.5.cloned.1.call-done, bf16[512,512]{1,0:T(8,128)(2,1)S(1)} %all_gather.19), kind=kOutput, calls=%fused_computation.1 | convolution fusion | flops 1074790400 | bytes 6815744 | tf_op jit(solution)/shard_map/dot_general | solution.py:99
  (21 shorter events, 1.0 us)
Async XLA Ops:
  7.2 161.2 %copy-start = (bf16[2048,512]{1,0:T(8,128)(2,1)S(1)}, bf16[2048,512]{1,0:T(8,128)(2,1)}, u32[]{:S(2)}) copy-start(bf16[2048,512]{1,0:T(8,128)(2,1)} %param.15) | copy-start | bytes 6291460
  7.2 35.5 %all-gather.3.cloned.1.call-start = ((), (), s32[]{:S(2)}) async-start(), calls=%async_computation.2 | async-start | bytes 1310720 | tf_op jit(solution)/shard_map/all_gather | solution.py:57
  24.2 93.1 %reduce-scatter.3.cloned.1.call-start = ((), (), s32[]{:S(2)}) async-start(), calls=%async_computation.3 | async-start | bytes 2359296 | tf_op jit(solution)/shard_map/reduce_scatter | solution.py:61
  48.8 68.5 %copy-start.2 = (bf16[64,2048]{1,0:T(8,128)(2,1)S(1)}, bf16[64,2048]{1,0:T(8,128)(2,1)}, u32[]{:S(2)}) copy-start(bf16[64,2048]{1,0:T(8,128)(2,1)} %param.14) | copy-start | bytes 786436
  48.9 119.5 %all-gather.5.cloned.1.call-start = ((), (), s32[]{:S(2)}) async-start(), calls=%async_computation.4 | async-start | bytes 2359296 | tf_op jit(solution)/shard_map/all_gather | solution.py:65
  119.1 53.1 %copy-start.1 = (bf16[128,4096]{1,0:T(8,128)(2,1)S(1)}, bf16[128,4096]{1,0:T(8,128)(2,1)}, u32[]{:S(2)}) copy-start(bf16[128,4096]{1,0:T(8,128)(2,1)} %param.16) | copy-start | bytes 3145732
  119.1 53.1 %copy-start.3 = (bf16[128,512]{1,0:T(8,128)(2,1)S(1)}, bf16[128,512]{1,0:T(8,128)(2,1)}, u32[]{:S(2)}) copy-start(bf16[128,512]{1,0:T(8,128)(2,1)} %param.17) | copy-start | bytes 393220
  119.1 76.6 %reduce-scatter.5.cloned.1.call-start = ((), (), s32[]{:S(2)}) async-start(), calls=%async_computation.5 | async-start | bytes 1310720 | tf_op jit(solution)/shard_map/reduce_scatter | solution.py:67
Sparse Core Ops, SparseCore 0:
  24.3 18.3 all-gather.2
  49.0 68.2 reduce-scatter.2
  120.0 48.2 all-gather.4
  172.3 23.3 reduce-scatter.4
where the time goes:
time: 398 us
  blocking collectives  207 us (52%)
  waiting for transfers between devices  136 us (34%)
  matrix products  26.1 us (7%)
  between operations  13.9 us (3%)
  local copies, waits for them, and re-layouts  8.21 us (2%)
  other arithmetic  5.7 us (1%)
    psum x1, blocking collectives, on_device(): weight_sum, gain_sum = lax.psum((weight_part, gain_part), 'mp')  147 us
    reduce_scatter x1, waiting for transfers between devices, on_device(): lax.psum_scatter(head_terms.astype(jnp.bfloat16), 'dp', scatter_dimension...  68.4 us
    all_gather x1, waiting for transfers between devices, on_device(): hidden_all = lax.all_gather(hidden, 'dp', axis=0, tiled=True)  49.2 us
    psum x1, blocking collectives, on_device(): inner = lax.psum(jnp.sum(upstream * state, axis=1), 'dp')  22 us
    psum x1, blocking collectives, on_device(): squares = lax.psum(jnp.sum(state * state, axis=1), 'dp')  18.9 us
    all_gather x1, waiting for transfers between devices, on_device(): lax.all_gather(context, 'mp', axis=0, tiled=True)  18.4 us
  transfers between devices with their start and end apart: 4, of which 4 were waited for; matrix products, arithmetic and copies ran while one was open for 1% of the time, Pallas kernels for 0%

commit v1 on v0

--- a/solution.py
+++ b/solution.py
@@ -32,10 +32,8 @@
     kv_start = dp_index * local_heads // groups
     key_mine = lax.dynamic_slice_in_dim(teacher_keys, kv_start * HEAD, kv_local * HEAD, 1)
     value_mine = lax.dynamic_slice_in_dim(teacher_values, kv_start * HEAD, kv_local * HEAD, 1)
-    keys_all, values_all = (
-        lax.all_gather(key_mine, "mp", axis=0, tiled=True),
-        lax.all_gather(value_mine, "mp", axis=0, tiled=True),
-    )
+    both = lax.all_gather(jnp.concatenate([key_mine, value_mine], 1), "mp", axis=0, tiled=True)
+    keys_all, values_all = both[:, : kv_local * HEAD], both[:, kv_local * HEAD :]
     total = keys_all.shape[0]
     repeat = local_heads // kv_local
     queries = teacher_query.reshape(query_rows, kv_local, repeat, HEAD)
@@ -63,6 +61,7 @@
     ).astype(jnp.float32)
     hidden = (teacher_resid.astype(jnp.float32) + summed).astype(jnp.bfloat16)
     hidden_all = lax.all_gather(hidden, "dp", axis=0, tiled=True)
+    student_all = lax.all_gather(student_context, "mp", axis=0, tiled=True)
     rows = hidden_all
     target = lax.psum_scatter(
         jnp.dot(rows, distill_proj, preferred_element_type=jnp.float32),
@@ -87,21 +86,20 @@
     gain_term = error * state * inverse
     grad_bf = grad_state.astype(jnp.bfloat16)
     error_bf = error.astype(jnp.bfloat16)
-    gain_part = jnp.sum(gain_term, axis=0)
+    gain_sum = lax.psum(jnp.sum(gain_term, axis=0), "mp")
     contract_rows = (((0,), (0,)), ((), ()))
-    weight_part = lax.dot_general(
-        student_context, grad_bf, contract_rows, preferred_element_type=jnp.float32
-    )
-    weight_sum, gain_sum = lax.psum((weight_part, gain_part), "mp")
-    grad_wo = weight_sum.astype(jnp.bfloat16)
-    empty = jnp.zeros((hidden_all.shape[1], columns), jnp.float32)
-    rows = hidden_all
-    grad_proj = empty - lax.dot_general(
+    grad_proj = -lax.dot_general(
         rows,
         lax.all_gather(error_bf, "mp", axis=0, tiled=True),
         contract_rows,
         preferred_element_type=jnp.float32,
     )
+    grad_wo = lax.dot_general(
+        student_all,
+        lax.all_gather(grad_bf, "mp", axis=0, tiled=True),
+        contract_rows,
+        preferred_element_type=jnp.float32,
+    ).astype(jnp.bfloat16)
     return (grad_wo, gain_sum, grad_proj)
 
 

time: 398 us -> 260 us (0.65)
  blocking collectives: 207 us -> 69 us
    psum x1, blocking collectives: 147 us -> 6.76 us  [on_device(): gain_sum = lax.psum(jnp.sum(gain_term, axis=0), 'mp')]
  transfers between devices with their start and end apart: 4 -> 5, of which waited for: 4 -> 3; matrix products, arithmetic and copies ran while one was open for 1% -> 2% of each run, Pallas kernels for 0% -> 0%
where the time goes in v1:
time: 260 us
  waiting for transfers between devices  136 us (52%)
  blocking collectives  69 us (27%)
  matrix products  27.1 us (10%)
  between operations  13.9 us (5%)
  local copies, waits for them, and re-layouts  7.93 us (3%)
  other arithmetic  5.12 us (2%)
    reduce_scatter x1, waiting for transfers between devices, on_device(): lax.psum_scatter(head_terms.astype(jnp.bfloat16), 'dp', scatter_dimension...  68.3 us
    all_gather x1, waiting for transfers between devices, on_device(): hidden_all = lax.all_gather(hidden, 'dp', axis=0, tiled=True)  49.2 us
    psum x1, blocking collectives, on_device(): inner = lax.psum(jnp.sum(upstream * state, axis=1), 'dp')  21 us
    psum x1, blocking collectives, on_device(): squares = lax.psum(jnp.sum(state * state, axis=1), 'dp')  18.9 us
    all_gather x1, waiting for transfers between devices, on_device(): lax.all_gather(context, 'mp', axis=0, tiled=True)  18.2 us
    all_gather x1, blocking collectives, on_device(): lax.all_gather(grad_bf, 'mp', axis=0, tiled=True)  7.79 us
    all_gather x1, blocking collectives, on_device(): lax.all_gather(error_bf, 'mp', axis=0, tiled=True)  7.28 us
    all_gather x1, blocking collectives, on_device(): lax.all_gather(jnp.concatenate([key_mine, value_mine], 1), 'mp', axis=0,...  7.22 us
  transfers between devices with their start and end apart: 5, of which 3 were waited for; matrix products, arithmetic and copies ran while one was open for 2% of the time, Pallas kernels for 0%

profile of v1, /device:TPU:0, one launch (start us, length us, event | category | flops | bytes accessed | tf_op | source)
XLA Modules:
  0.0 259.6 jit_solution(2404129158851385705)
XLA Ops:
  7.3 0.9 constant_dynamic-slice_fusion
  8.2 7.2 %all_gather.18 = bf16[512,256]{1,0:T(8,128)(2,1)S(1)} all-gather(bf16[128,256]{1,0:T(8,128)(2,1)S(1)} %pad_maximum_fusion), channel_id=1, replica_groups=mesh['dp'=8,'mp'=4] {'mp'}, dimensions={0}, use_global_device_ids=true | all-gather | bytes 327680 | tf_op jit(solution)/shard_map/all_gather | solution.py:35
  15.5 1.4 fusion.5
  17.2 1.2 convolution_convert_fusion.2
  18.5 18.2 %all-gather.4.cloned.1.call-done = bf16[512,1024]{0,1:T(8,128)(2,1)} async-done(((bf16[128,1024]{0,1:T(8,128)(2,1)}), bf16[512,1024]{0,1:T(8,128)(2,1)}) %all-gather.4.cloned.1.call-update) | async-done | bytes 1048592 | tf_op jit(solution)/shard_map/all_gather | solution.py:55
  36.7 6.2 %convolution_convert_fusion.1 = bf16[512,2048]{1,0:T(8,128)(2,1)} fusion(bf16[512,1024]{0,1:T(8,128)(2,1)} %all-gather.4.cloned.1.call-done, bf16[1024,2048]{1,0:T(8,128)(2,1)} %param.13), kind=kOutput, calls=%fused_computation.3 | convolution fusion | flops 2148532224 | bytes 7340032 | tf_op jit(solution)/shard_map/dot_general | solution.py:54
  43.0 68.3 %reduce-scatter.3.cloned.1.call-done = bf16[64,2048]{1,0:T(8,128)(2,1)} async-done(((bf16[512,2048]{1,0:T(8,128)(2,1)}), bf16[64,2048]{1,0:T(8,128)(2,1)}) %reduce-scatter.3.cloned.1.call-update) | async-done | bytes 262160 | tf_op jit(solution)/shard_map/reduce_scatter | solution.py:59
  111.3 1.7 add_convert_fusion
  113.1 49.2 %all-gather.6.cloned.1.call-done = bf16[512,2048]{1,0:T(8,128)(2,1)} async-done(((bf16[64,2048]{1,0:T(8,128)(2,1)}), bf16[512,2048]{1,0:T(8,128)(2,1)}) %all-gather.6.cloned.1.call-update) | async-done | bytes 2097168 | tf_op jit(solution)/shard_map/all_gather | solution.py:63
  162.3 3.8 %fusion.6 = f32[512,512]{1,0:T(8,128)} fusion(bf16[512,2048]{1,0:T(8,128)(2,1)} %all-gather.6.cloned.1.call-done, bf16[2048,512]{1,0:T(8,128)(2,1)S(1)} %copy-done), kind=kOutput, calls=%fused_computation.32 | convolution fusion | flops 1073741824 | bytes 5242880 | tf_op jit(solution)/shard_map/dot_general | solution.py:67
  166.2 0.5 all-gather.8.cloned.1.call-update
  166.7 0.6 copy-done.1
  167.3 3.0 %multiply_reduce_fusion.2 = (f32[128]{0:T(128)S(1)}, f32[128,512]{1,0:T(8,128)S(1)}) fusion(bf16[128,4096]{1,0:T(8,128)(2,1)S(1)} %copy-done.1, bf16[4096,512]{1,0:T(8,128)(2,1)} %param.18, bf16[128,512]{1,0:T(8,128)(2,1)S(1)} %copy-done.3), kind=kOutput, calls=%fused_computation.19 | convolution fusion | flops 537132928 | bytes 5636608 | tf_op jit(solution)/shard_map/dot_general | solution.py:74
  170.3 18.9 %psum.21 = f32[128]{0:T(128)S(1)} all-reduce(f32[128]{0:T(128)S(1)} %get-tuple-element.13), channel_id=1, replica_groups=mesh['dp'=8,'mp'=4] {'dp'}, use_global_device_ids=true, to_apply=%region_1.2 | all-reduce | flops 128 | bytes 1024 | tf_op jit(solution)/shard_map/psum | solution.py:79
  189.2 0.8 broadcast_multiply_fusion
  190.0 1.2 multiply_reduce_fusion
  191.2 21.0 %psum.22 = f32[128]{0:T(128)S(1)} all-reduce(f32[128]{0:T(128)S(1)} %get-tuple-element.7), channel_id=1, replica_groups=mesh['dp'=8,'mp'=4] {'dp'}, use_global_device_ids=true, to_apply=%region_7.8 | all-reduce | flops 128 | bytes 1024 | tf_op jit(solution)/shard_map/psum | solution.py:84
  212.2 6.8 %psum.23 = f32[512]{0:T(512)} all-reduce(f32[512]{0:T(512)S(1)} %get-tuple-element.6), channel_id=1, replica_groups=mesh['dp'=8,'mp'=4] {'mp'}, use_global_device_ids=true, to_apply=%region_9.10 | all-reduce | flops 512 | bytes 4096 | tf_op jit(solution)/shard_map/psum | solution.py:89
  219.0 1.1 subtract_convert_fusion
  220.1 7.8 %all_gather.21 = bf16[512,512]{1,0:T(8,128)(2,1)S(1)} all-gather(bf16[128,512]{1,0:T(8,128)(2,1)S(1)} %subtract_convert_fusion), channel_id=1, replica_groups=mesh['dp'=8,'mp'=4] {'mp'}, dimensions={0}, use_global_device_ids=true | all-gather | bytes 655360 | tf_op jit(solution)/shard_map/all_gather | solution.py:99
  227.9 6.6 %fusion = bf16[4096,512]{0,1:T(8,128)(2,1)} fusion(bf16[512,512]{1,0:T(8,128)(2,1)S(1)} %all_gather.21, bf16[512,4096]{1,0:T(8,128)(2,1)} %all-gather.8.cloned.1.call-done), kind=kOutput, calls=%fused_computation.1 | convolution fusion | flops 2149580800 | bytes 8912896 | tf_op jit(solution)/shard_map/dot_general | solution.py:97
  234.4 6.4 %copy.16 = bf16[4096,512]{1,0:T(8,128)(2,1)} copy(bf16[4096,512]{0,1:T(8,128)(2,1)} %fusion) | data formatting | bytes 8388608
  240.8 7.3 %all_gather.23 = bf16[512,512]{1,0:T(8,128)(2,1)S(1)} all-gather(bf16[128,512]{1,0:T(8,128)(2,1)S(1)} %get-tuple-element.10), channel_id=1, replica_groups=mesh['dp'=8,'mp'=4] {'mp'}, dimensions={0}, use_global_device_ids=true | all-gather | bytes 655360 | tf_op jit(solution)/shard_map/all_gather | solution.py:93
  248.1 4.9 %convolution_negate_fusion = f32[2048,512]{1,0:T(8,128)} fusion(bf16[512,2048]{1,0:T(8,128)(2,1)} %all-gather.6.cloned.1.call-done, bf16[512,512]{1,0:T(8,128)(2,1)S(1)} %all_gather.23), kind=kOutput, calls=%fused_computation.2 | convolution fusion | flops 1074790400 | bytes 6815744 | tf_op jit(solution)/shard_map/dot_general | solution.py:91
  (24 shorter events, 0.7 us)
Async XLA Ops:
  7.2 155.1 %copy-start = (bf16[2048,512]{1,0:T(8,128)(2,1)S(1)}, bf16[2048,512]{1,0:T(8,128)(2,1)}, u32[]{:S(2)}) copy-start(bf16[2048,512]{1,0:T(8,128)(2,1)} %param.15) | copy-start | bytes 6291460
  7.2 29.5 %all-gather.4.cloned.1.call-start = ((), (), s32[]{:S(2)}) async-start(), calls=%async_computation.2 | async-start | bytes 1310720 | tf_op jit(solution)/shard_map/all_gather | solution.py:55
  18.4 92.9 %reduce-scatter.3.cloned.1.call-start = ((), (), s32[]{:S(2)}) async-start(), calls=%async_computation.3 | async-start | bytes 2359296 | tf_op jit(solution)/shard_map/reduce_scatter | solution.py:59
  42.9 68.4 %copy-start.2 = (bf16[64,2048]{1,0:T(8,128)(2,1)S(1)}, bf16[64,2048]{1,0:T(8,128)(2,1)}, u32[]{:S(2)}) copy-start(bf16[64,2048]{1,0:T(8,128)(2,1)} %param.14) | copy-start | bytes 786436
  42.9 119.3 %all-gather.6.cloned.1.call-start = ((), (), s32[]{:S(2)}) async-start(), calls=%async_computation.4 | async-start | bytes 2359296 | tf_op jit(solution)/shard_map/all_gather | solution.py:63
  113.0 77.0 %reduce-scatter.5.cloned.1.call-start = ((), (), s32[]{:S(2)}) async-start(), calls=%async_computation.5 | async-start | bytes 1310720 | tf_op jit(solution)/shard_map/reduce_scatter | solution.py:66
  166.1 1.2 copy-start.1
  166.1 1.2 copy-start.3
  166.1 61.7 %all-gather.8.cloned.1.call-start = ((), (), s32[]{:S(2)}) async-start(), calls=%async_computation.6 | async-start | bytes 5242880 | tf_op jit(solution)/shard_map/all_gather | solution.py:64
Sparse Core Ops, SparseCore 0:
  18.5 18.1 all-gather.3
  43.1 68.1 reduce-scatter.2
  114.0 48.2 all-gather.5
  166.2 23.3 reduce-scatter.4
  191.2 35.7 all-gather.7

commit v2 on v1

v2 whole, which is shorter than its diff:
```python
import functools

import jax
import jax.numpy as jnp
from jax import lax
from jax.experimental import pallas as pl
from jax.experimental.pallas import tpu as pltpu
from jax.sharding import PartitionSpec as P

HEADS = 64
KV_HEADS = 8
HEAD = 128
EPS = 1e-05
MESH = pl.DeviceIdType.MESH
F32 = jnp.float32
BF16 = jnp.bfloat16


def position_of(index, n):
    z, x = index // 2, index % 2
    return z + x * (n - 1 - 2 * z)


def index_at(position, n):
    side = position // (n // 2)
    return 2 * (position + side * (n - 1 - 2 * position)) + side


class Gather:
    def __init__(self, block, mine, mn, mp, sends, recvs, passes, own=None):
        self.block, self.mine, self.mn, self.mp, self.own = block, mine, mn, mp, own
        self.sends, self.recvs, self.passes = sends, recvs, passes
        self.core, self.group, self.groups = mp % 2, mp // 2, mn // 2
        self.sibling = self.group * 2 + (1 - self.core)

    def same(self, j):
        return ((self.group + j) % self.groups) * 2 + self.core

    def other(self, j):
        return ((self.group + j) % self.groups) * 2 + (1 - self.core)

    def copy(self, source, who, send_sem, target):
        return pltpu.make_async_remote_copy(
            src_ref=source,
            dst_ref=self.block(who),
            send_sem=send_sem,
            recv_sem=self.recvs.at[who],
            device_id={"mp": target},
            device_id_type=MESH,
        )

    def first(self, j):
        target = self.same(j) if j else self.sibling
        return self.copy(self.mine, self.mp, self.sends.at[j], target)

    def start(self):
        for j in range(self.groups):
            self.first(j).start()

    def passed(self, j):
        who = self.same(j)
        return self.copy(self.block(who), who, self.passes.at[j], self.sibling)

    def forward(self):
        for j in range(1, self.groups):
            self.passed(j).wait_recv()
            self.passed(j).start()

    def finish(self):
        for j in range(self.groups):
            who = self.other(j)
            self.copy(self.block(who), who, self.sends.at[j], self.sibling).wait_recv()
        for j in range(self.groups):
            self.first(j).wait_send()
        for j in range(1, self.groups):
            self.passed(j).wait_send()


def to_columns(row, rows, width):
    tile = jnp.transpose(jnp.broadcast_to(row, (128, rows)))
    return jnp.concatenate([tile] * (width // 128), axis=1) if width > 128 else tile


def sum_to_row(values):
    ones = jnp.ones((8, values.shape[1]), F32)
    return lax.dot_general(
        ones, values, (((1,), (1,)), ((), ())),
        precision=lax.Precision.HIGHEST, preferred_element_type=F32,
    )


def middle(
    n, mn, width, tokens,
    ctx, tout_hbm, resid, proj_hbm, sctx_hbm, sresid, sout_hbm, gain,
    hid_out, sall_out, err_out, st_out, coef_out,
    tout, proj, sctx, sout, head, hid, rs, tsend, trecv, err, st, state, sq, inn, coef,
    load, store, rs_send, rs_recv, ag_send, ag_recv, t_send, t_recv,
    sq_send, sq_recv, in_send, in_recv, co_send, co_recv,
    s_send, s_recv, s_pass, st_send, st_recv, st_pass, e_send, e_recv, e_pass,
):
    d, m = lax.axis_index("dp"), lax.axis_index("mp")
    rows = tokens // mn
    shard = tokens // n
    half = shard // 2
    per = n // mn
    features = proj.shape[0]
    columns = proj.shape[1]
    p = position_of(d, n)

    loads = [
        pltpu.make_async_copy(src, dst, load.at[i])
        for i, (src, dst) in enumerate(
            ((tout_hbm, tout), (sctx_hbm, sctx), (sout_hbm, sout), (proj_hbm, proj))
        )
    ]
    for one in loads:
        one.start()

    barrier = pltpu.get_barrier_semaphore()
    for j in range(1, n):
        pl.semaphore_signal(barrier, inc=1, device_id={"dp": (d + j) % n}, device_id_type=MESH)
    for j in range(1, mn):
        pl.semaphore_signal(barrier, inc=1, device_id={"mp": (m + j) % mn}, device_id_type=MESH)
    pl.semaphore_wait(barrier, n - 1 + mn - 1)

    def block_of(ref):
        return lambda who: ref.at[pl.ds(pl.multiple_of(who * rows, rows), rows), :]

    my_rows = pl.ds(pl.multiple_of(m * rows, rows), rows)
    student = Gather(block_of(sall_out), sctx_hbm, mn, m, s_send, s_recv, s_pass)
    student.start()
    keep = pltpu.make_async_copy(sctx_hbm, sall_out.at[my_rows, :], store.at[0])
    keep.start()

    loads[0].wait()
    tile = min(512, features)

    @pl.loop(0, features // tile)
    def _(i):
        cols = pl.ds(pl.multiple_of(i * tile, tile), tile)
        head[:, cols] = jnp.dot(ctx[...], tout[:, cols], preferred_element_type=F32).astype(BF16)

    def chunk(position, way):
        start = index_at(position, n) * shard + way * half
        return pl.ds(pl.multiple_of(start, half), half)

    def toward(way):
        return index_at((p + 1 - 2 * way + n) % n, n)

    def sign(way):
        return 1 - 2 * way

    def reduce_copy(s, way):
        c = (p - sign(way) * (s + 1) + 2 * n) % n
        return pltpu.make_async_remote_copy(
            src_ref=head.at[chunk(c, way), :],
            dst_ref=rs.at[way, s],
            send_sem=rs_send.at[way, s],
            recv_sem=rs_recv.at[way, s],
            device_id={"dp": toward(way)},
            device_id_type=MESH,
        )

    for way in (0, 1):
        reduce_copy(0, way).start()

    def exchange(buf, sends, recvs, j):
        return pltpu.make_async_remote_copy(
            src_ref=buf.at[d],
            dst_ref=buf.at[d],
            send_sem=sends.at[j],
            recv_sem=recvs.at[d],
            device_id={"dp": (d + j) % n},
            device_id_type=MESH,
        )

    def exchange_wait(buf, sends, recvs):
        for j in range(1, n):
            who = (d + j) % n
            pltpu.make_async_remote_copy(
                src_ref=buf.at[who], dst_ref=buf.at[who], send_sem=sends.at[j],
                recv_sem=recvs.at[who], device_id={"dp": who}, device_id_type=MESH,
            ).wait_recv()
        for j in range(1, n):
            exchange(buf, sends, recvs, j).wait_send()

    def total_of(buf):
        whole = buf[0]
        for j in range(1, n):
            whole = whole + buf[j]
        return whole

    def reduce_step(s):
        for way in (0, 1):
            reduce_copy(s - 1, way).wait_recv()
            c = (p - sign(way) * (s + 1) + 2 * n) % n
            where = chunk(c, way)
            head[where, :] = (head[where, :].astype(F32) + rs[way, s - 1].astype(F32)).astype(BF16)
            reduce_copy(s, way).start()

    reduce_step(1)

    loads[1].wait()
    loads[2].wait()
    state[...] = sresid[...].astype(F32) + jnp.dot(sctx[...], sout[...], preferred_element_type=F32)
    st[my_rows, :] = state[...].astype(BF16)
    sq[d] = sum_to_row(state[...] * state[...])
    for j in range(1, n):
        exchange(sq, sq_send, sq_recv, j).start()
    states = Gather(block_of(st), st.at[my_rows, :], mn, m, st_send, st_recv, st_pass)
    states.start()

    @pl.loop(2, n - 1)
    def _(s):
        reduce_step(s)

    for way in (0, 1):
        reduce_copy(n - 2, way).wait_recv()
        where = chunk(p, way)
        mine = pl.ds(way * half, half)
        summed = head[where, :].astype(F32) + rs[way, n - 2].astype(F32)
        hid[where, :] = (resid[mine, :].astype(F32) + summed).astype(BF16)

    def gather_copy(s, way):
        where = chunk((p - sign(way) * s + 2 * n) % n, way)
        return pltpu.make_async_remote_copy(
            src_ref=hid.at[where, :],
            dst_ref=hid.at[where, :],
            send_sem=ag_send.at[way, s],
            recv_sem=ag_recv.at[way, s],
            device_id={"dp": toward(way)},
            device_id_type=MESH,
        )

    def arrival(s, way):
        where = chunk((p - sign(way) * (s + 1) + 2 * n) % n, way)
        return pltpu.make_async_remote_copy(
            src_ref=hid.at[where, :],
            dst_ref=hid.at[where, :],
            send_sem=ag_send.at[way, s],
            recv_sem=ag_recv.at[way, s],
            device_id={"dp": toward(way)},
            device_id_type=MESH,
        )

    def target_copy(owner, way):
        to = owner // per
        piece = pl.ds(pl.multiple_of((owner % per) * shard + way * half, half), half)
        start = pl.ds(pl.multiple_of(owner * shard + way * half, half), half)
        return pltpu.make_async_remote_copy(
            src_ref=tsend.at[start, :],
            dst_ref=trecv.at[m, piece, :],
            send_sem=t_send.at[way, owner],
            recv_sem=t_recv.at[m, way, owner % per],
            device_id={"mp": to},
            device_id_type=MESH,
        )

    def project(s):
        where = [chunk((p - sign(way) * s + 2 * n) % n, way) for way in (0, 1)]
        both = jnp.concatenate([hid[w, :] for w in where], axis=0)
        out = jnp.dot(both, proj[...], preferred_element_type=F32).astype(BF16)
        for way in (0, 1):
            tsend[where[way], :] = out[way * half : (way + 1) * half]
            owner = index_at((p - sign(way) * s + 2 * n) % n, n)

            @pl.when(owner // per != m)
            def _():
                target_copy(owner, way).start()

    for way in (0, 1):
        gather_copy(0, way).start()
    loads[3].wait()
    student.forward()
    states.forward()
    project(0)

    @pl.loop(1, n - 1)
    def _(s):
        for way in (0, 1):
            arrival(s - 1, way).wait_recv()
            gather_copy(s, way).start()
        project(s)

    for way in (0, 1):
        arrival(n - 2, way).wait_recv()
    project(n - 1)
    hid_store = pltpu.make_async_copy(hid, hid_out, store.at[1])
    hid_store.start()

    exchange_wait(sq, sq_send, sq_recv)
    inverse_row = lax.rsqrt(total_of(sq) / width + EPS)
    inverse = to_columns(inverse_row[0:1], rows, columns)
    pred = state[...] * inverse * gain[...]

    target = tsend[my_rows, :].astype(F32)
    for j in range(1, mn):
        who = (m + j) % mn
        for way in (0, 1):
            for k in range(per):
                piece = pl.ds(k * shard + way * half, half)
                pltpu.make_async_remote_copy(
                    src_ref=trecv.at[who, piece, :],
                    dst_ref=trecv.at[who, piece, :],
                    send_sem=t_send.at[way, k],
                    recv_sem=t_recv.at[who, way, k],
                    device_id={"mp": who},
                    device_id_type=MESH,
                ).wait_recv()
        target = target + trecv[who].astype(F32)

    error = (pred - target) * (tokens ** -0.5)
    err[my_rows, :] = error.astype(BF16)
    errors = Gather(block_of(err), err.at[my_rows, :], mn, m, e_send, e_recv, e_pass)
    errors.start()
    inn[d] = sum_to_row(error * gain[...] * state[...])
    for j in range(1, n):
        exchange(inn, in_send, in_recv, j).start()

    states.finish()
    st_store = pltpu.make_async_copy(st, st_out, store.at[2])
    st_store.start()
    student.finish()

    exchange_wait(inn, in_send, in_recv)
    inner_row = total_of(inn)
    coef[m, 0:8, :] = inverse_row
    coef[m, 8:16, :] = inverse_row * inverse_row * inverse_row * (inner_row / width)

    def coef_copy(j):
        return pltpu.make_async_remote_copy(
            src_ref=coef.at[m], dst_ref=coef.at[m], send_sem=co_send.at[j],
            recv_sem=co_recv.at[m], device_id={"mp": (m + j) % mn}, device_id_type=MESH,
        )

    for j in range(1, mn):
        coef_copy(j).start()
    errors.forward()
    errors.finish()
    err_store = pltpu.make_async_copy(err, err_out, store.at[3])
    err_store.start()
    for j in range(1, mn):
        who = (m + j) % mn
        pltpu.make_async_remote_copy(
            src_ref=coef.at[who], dst_ref=coef.at[who], send_sem=co_send.at[j],
            recv_sem=co_recv.at[who], device_id={"mp": who}, device_id_type=MESH,
        ).wait_recv()
    for j in range(1, mn):
        coef_copy(j).wait_send()
    coef_out[...] = coef[...]

    @pl.loop(0, n - 1)
    def _(s):
        for way in (0, 1):
            reduce_copy(s, way).wait_send()
            gather_copy(s, way).wait_send()

    @pl.loop(0, n)
    def _(owner):
        @pl.when(owner // per != m)
        def _():
            for way in (0, 1):
                target_copy(owner, way).wait_send()

    keep.wait()
    hid_store.wait()
    st_store.wait()
    err_store.wait()


def on_device(
    n,
    mn,
    teacher_query,
    teacher_keys,
    teacher_values,
    teacher_out,
    teacher_resid,
    distill_proj,
    student_context,
    student_resid,
    student_out,
    student_gain,
):
    groups = HEADS // KV_HEADS
    dp_index = lax.axis_index("dp")
    mp_index = lax.axis_index("mp")
    query_rows, query_width = teacher_query.shape
    local_heads = query_width // HEAD
    kv_local = max(local_heads // groups, 1)
    kv_start = dp_index * local_heads // groups
    key_mine = lax.dynamic_slice_in_dim(teacher_keys, kv_start * HEAD, kv_local * HEAD, 1)
    value_mine = lax.dynamic_slice_in_dim(teacher_values, kv_start * HEAD, kv_local * HEAD, 1)
    both = lax.all_gather(jnp.concatenate([key_mine, value_mine], 1), "mp", axis=0, tiled=True)
    keys_all, values_all = both[:, : kv_local * HEAD], both[:, kv_local * HEAD :]
    total = keys_all.shape[0]
    repeat = local_heads // kv_local
    queries = teacher_query.reshape(query_rows, kv_local, repeat, HEAD)
    keyed = keys_all.reshape(total, kv_local, HEAD)
    valued = values_all.reshape(total, kv_local, HEAD)
    scores = jnp.einsum(
        "qgrd,kgd->grqk", queries, keyed, preferred_element_type=jnp.float32
    ) * HEAD ** (-0.5)
    query_pos = mp_index * query_rows + lax.iota(jnp.int32, query_rows)
    key_pos = lax.iota(jnp.int32, total)
    allowed = query_pos[:, None] >= key_pos[None, :]
    scores = jnp.where(allowed, scores, -jnp.inf)
    top = jnp.max(scores, axis=-1, keepdims=True)
    weights = jnp.exp(scores - top)
    probs = (weights / jnp.sum(weights, axis=-1, keepdims=True)).astype(jnp.bfloat16)
    context = jnp.einsum("grqk,kgd->qgrd", probs, valued, preferred_element_type=jnp.float32)
    context = context.astype(jnp.bfloat16).reshape(query_rows, query_width)
    context_all = lax.all_gather(context, "mp", axis=0, tiled=True)

    features, columns = distill_proj.shape
    width = student_context.shape[1]
    shard = total // n
    rows = total // mn
    gain = lax.dynamic_slice_in_dim(student_gain, dp_index * columns, columns, 0).reshape(1, columns)
    vmem = pl.BlockSpec(memory_space=pltpu.VMEM)
    anywhere = pl.BlockSpec(memory_space=pl.ANY)
    dma = pltpu.SemaphoreType.DMA
    pairs = mn // 2
    hidden, student_all, error, state, coef = pl.pallas_call(
        functools.partial(middle, n, mn, width, total),
        out_shape=(
            jax.ShapeDtypeStruct((total, features), BF16),
            jax.ShapeDtypeStruct((total, width), BF16),
            jax.ShapeDtypeStruct((total, columns), BF16),
            jax.ShapeDtypeStruct((total, columns), BF16),
            jax.ShapeDtypeStruct((mn, 16, rows), F32),
        ),
        in_specs=[vmem, anywhere, vmem, anywhere, anywhere, vmem, anywhere, vmem],
        out_specs=(anywhere, anywhere, anywhere, anywhere, vmem),
        scratch_shapes=[
            pltpu.VMEM(teacher_out.shape, BF16),
            pltpu.VMEM(distill_proj.shape, BF16),
            pltpu.VMEM(student_context.shape, BF16),
            pltpu.VMEM(student_out.shape, BF16),
            pltpu.VMEM((total, features), BF16),
            pltpu.VMEM((total, features), BF16),
            pltpu.VMEM((2, n - 1, shard // 2, features), BF16),
            pltpu.VMEM((total, columns), BF16),
            pltpu.VMEM((mn, rows, columns), BF16),
            pltpu.VMEM((total, columns), BF16),
            pltpu.VMEM((total, columns), BF16),
            pltpu.VMEM((rows, columns), F32),
            pltpu.VMEM((n, 8, rows), F32),
            pltpu.VMEM((n, 8, rows), F32),
            pltpu.VMEM((mn, 16, rows), F32),
            dma((4,)),
            dma((4,)),
            dma((2, n - 1)),
            dma((2, n - 1)),
            dma((2, n - 1)),
            dma((2, n - 1)),
            dma((2, n)),
            dma((mn, 2, n // mn)),
            dma((n,)), dma((n,)), dma((n,)), dma((n,)),
            dma((mn,)), dma((mn,)),
            dma((pairs,)), dma((mn,)), dma((pairs,)),
            dma((pairs,)), dma((mn,)), dma((pairs,)),
            dma((pairs,)), dma((mn,)), dma((pairs,)),
        ],
        compiler_params=pltpu.CompilerParams(
            collective_id=0, has_side_effects=True, vmem_limit_bytes=48 * 1024 * 1024
        ),
        name="middle",
    )(
        context_all, teacher_out, teacher_resid, distill_proj,
        student_context, student_resid, student_out, gain,
    )
    inverse = coef[:, 0, :].reshape(total, 1)
    pull = coef[:, 8, :].reshape(total, 1)
    wide = error.astype(F32) * inverse
    kept = state.astype(F32)
    grad_gain = jnp.sum(wide * kept, axis=0)
    grad_state = (wide * gain - kept * pull).astype(BF16)
    contract_rows = (((0,), (0,)), ((), ()))
    grad_proj = -lax.dot_general(hidden, error, contract_rows, preferred_element_type=F32)
    grad_wo = lax.dot_general(
        student_all, grad_state, contract_rows, preferred_element_type=F32
    ).astype(BF16)
    return (grad_wo, grad_gain, grad_proj)


def solution(mesh):
    in_specs = (
        P("mp", "dp"),
        P("mp", None),
        P("mp", None),
        P("dp", "mp"),
        P("dp", "mp"),
        P("mp", "dp"),
        P("mp", None),
        P("mp", "dp"),
        P(None, "dp"),
        P(),
    )
    out_specs = (P(None, "dp"), P("dp"), P("mp", "dp"))
    return jax.shard_map(
        functools.partial(on_device, mesh.shape["dp"], mesh.shape["mp"]),
        mesh=mesh, in_specs=in_specs, out_specs=out_specs, check_vma=False,
    )
```

time: 260 us -> 138 us (0.53)
  waiting for transfers between devices: 136 us -> 17.4 us
  Pallas kernels: 0 us -> 84.8 us
  blocking collectives: 69 us -> 7.22 us
  matrix products: 27.1 us -> 8.91 us
  local copies, waits for them, and re-layouts: 7.93 us -> 3.66 us
  other arithmetic: 5.12 us -> 1.18 us
    pallas_call x0 -> x1, Pallas kernels: none -> 84.8 us  [on_device(): pl.pallas_call(functools.partial(middle, n, mn, width, total), out_shape=...]
    reduce_scatter x2 -> x0, waiting for transfers between devices: 68.3 us -> none  [the longest x1 68.3 us: on_device(): lax.psum_scatter(head_terms.astype(jnp.bfloat16), 'dp', scatter_dimension...]
    all_gather x3 -> x1, waiting for transfers between devices: 67.5 us -> 17.4 us  [on_device(): context_all = lax.all_gather(context, 'mp', axis=0, tiled=True)]
    psum x3 -> x0, blocking collectives: 46.7 us -> none  [the longest x1 21 us: on_device(): inner = lax.psum(jnp.sum(upstream * state, axis=1), 'dp')]
    dot_general x5 -> x2, matrix products: 24.5 us -> 7.94 us  [the longest x1 4.62 us: on_device(): lax.dot_general(student_all, grad_state, contract_rows, preferred_element...]
    all_gather x2 -> x0, blocking collectives: 15.1 us -> none  [the longest x1 7.79 us: on_device(): lax.all_gather(grad_bf, 'mp', axis=0, tiled=True)]
    unnamed x9 -> x12, local copies, waits for them, and re-layouts: 7.02 us -> 1.26 us
    convert_element_type x2 -> x0, other arithmetic: 2.81 us -> none  [the longest x1 1.71 us: on_device(): hidden = (teacher_resid.astype(jnp.float32) + summed).astype(jnp.bfloat16)]
  transfers between devices with their start and end apart: 5 -> 1, of which waited for: 3 -> 1; matrix products, arithmetic and copies ran while one was open for 2% -> 1% of each run, Pallas kernels for 0% -> 0%
where the time goes in v2:
time: 138 us; the launch traced here: 137 us
  Pallas kernels  84.8 us (61%)
  waiting for transfers between devices  17.4 us (13%)
  between operations  14.2 us (10%)
  matrix products  8.91 us (6%)
  blocking collectives  7.22 us (5%)
  local copies, waits for them, and re-layouts  3.66 us (3%)
    pallas_call x1, Pallas kernels, on_device(): pl.pallas_call(functools.partial(middle, n, mn, width, total), out_shape=...  84.8 us
    all_gather x1, waiting for transfers between devices, on_device(): context_all = lax.all_gather(context, 'mp', axis=0, tiled=True)  17.4 us
    all_gather x1, blocking collectives, on_device(): lax.all_gather(jnp.concatenate([key_mine, value_mine], 1), 'mp', axis=0,...  7.22 us
    dot_general x1, matrix products, on_device(): lax.dot_general(student_all, grad_state, contract_rows, preferred_element...  4.62 us
    dot_general x1, matrix products, on_device(): lax.dot_general(hidden, error, contract_rows, preferred_element_type=F32)  3.32 us
  transfers between devices with their start and end apart: 1, of which 1 were waited for; matrix products, arithmetic and copies ran while one was open for 1% of the time, Pallas kernels for 0%

profile of v2, /device:TPU:0, one launch (start us, length us, event | category | flops | bytes accessed | tf_op | source)
XLA Modules:
  0.0 137.4 jit_solution(7032994960722519762)
XLA Ops:
  7.2 0.0 copy-start
  7.2 0.0 all-gather.2.cloned.1.call-start
  7.3 0.8 constant_dynamic-slice_fusion
  8.1 7.2 %all_gather.6 = bf16[512,256]{1,0:T(8,128)(2,1)S(1)} all-gather(bf16[128,256]{1,0:T(8,128)(2,1)S(1)} %pad_maximum_fusion), channel_id=1, replica_groups=mesh['dp'=8,'mp'=4] {'mp'}, dimensions={0}, use_global_device_ids=true | all-gather | bytes 327680 | tf_op jit(solution)/shard_map/all_gather | solution.py:394
  15.3 0.0 copy-done
  15.3 0.4 fusion.12
  15.8 0.3 fusion
  16.1 0.0 copy-start.1
  16.1 0.0 copy-start.3
  16.1 0.0 copy-start.4
  16.1 0.5 convolution_convert_fusion.1
  16.7 0.9 copy.20
  17.5 0.0 all-gather.2.cloned.1.call-update
  17.5 0.8 dynamic_slice.11
  18.3 17.4 %all-gather.2.cloned.1.call-done.ctx = bf16[512,1024]{1,0:T(8,128)(2,1)} async-done(((bf16[128,1024]{1,0:T(8,128)(2,1)}), bf16[512,1024]{1,0:T(8,128)(2,1)}) %all-gather.2.cloned.1.call-update) | async-done | bytes 1048592 | tf_op jit(solution)/shard_map/all_gather | solution.py:413
  35.7 0.0 copy-done.1
  35.7 0.0 copy-done.3
  35.7 0.0 copy-done.4
  35.7 1.2 copy-done.2
  37.0 84.8 %middle.1 = (bf16[512,2048]{1,0:T(8,128)(2,1)S(1)}, bf16[512,4096]{1,0:T(8,128)(2,1)}, bf16[512,512]{1,0:T(8,128)(2,1)S(1)}, bf16[512,512]{1,0:T(8,128)(2,1)S(1)}, f32[4,16,128]{2,1,0:T(8,128)S(1)}) custom-call(bf16[512,1024]{1,0:T(8,128)(2,1)S(1)} %copy-done.2, bf16[1024,2048]{1,0:T(8,128)(2,1)} %tout_hbm.1, bf16[64,2048]{1,0:T(8,128)(2,1)S(1)} %copy-done.3, ...), custom_call_target="tpu_custom_call" | custom-call | tf_op jit(solution)/shard_map/middle/pallas_call | solution.py:424
  121.8 0.0 copy-start.5
  121.8 3.3 %convolution_negate_fusion = f32[2048,512]{1,0:T(8,128)} fusion(bf16[512,2048]{1,0:T(8,128)(2,1)S(1)} %get-tuple-element.12, bf16[512,512]{1,0:T(8,128)(2,1)S(1)} %get-tuple-element.9), kind=kOutput, calls=%fused_computation.1 | convolution fusion | flops 1074790400 | bytes 6815744 | tf_op jit(solution)/shard_map/dot_general | solution.py:480
  125.1 0.8 fusion.3
  126.0 4.6 %convolution_convert_fusion = bf16[4096,512]{1,0:T(8,128)(2,1)} fusion(bf16[512,4096]{1,0:T(8,128)(2,1)S(1)} %copy-done.5, bf16[512,512]{1,0:T(8,128)(2,1)S(1)} %get-tuple-element.11, bf16[512,512]{1,0:T(8,128)(2,1)S(1)} %get-tuple-element.9, f32[512]{0:T(512)S(1)} %bitcast.39, f32[512]{0:T(512)S(1)} %dynamic_slice.11, f32[512]{0:T(512)S(1)} %bitcast.38), kind=kOutput, calls=%fused_computation | convolution fusion | flops 2151415808 | bytes 9443328 | tf_op jit(solution)/shard_map/dot_general | solution.py:481
  (6 shorter events, 0.1 us)
Async XLA Ops:
  7.2 8.2 %copy-start = (bf16[128,1024]{1,0:T(8,128)(2,1)S(1)}, bf16[128,1024]{1,0:T(8,128)(2,1)}, u32[]{:S(2)}) copy-start(bf16[128,1024]{1,0:T(8,128)(2,1)} %param.10) | copy-start | bytes 786436
  7.2 28.5 %all-gather.2.cloned.1.call-start = ((), (), s32[]{:S(2)}) async-start(), calls=%async_computation | async-start | bytes 1310720 | tf_op jit(solution)/shard_map/all_gather | solution.py:413
  16.1 19.6 %copy-start.1 = (bf16[128,4096]{1,0:T(8,128)(2,1)S(1)}, bf16[128,4096]{1,0:T(8,128)(2,1)}, u32[]{:S(2)}) copy-start(bf16[128,4096]{1,0:T(8,128)(2,1)} %sctx_hbm.1) | copy-start | bytes 3145732
  16.1 19.6 %copy-start.3 = (bf16[64,2048]{1,0:T(8,128)(2,1)S(1)}, bf16[64,2048]{1,0:T(8,128)(2,1)}, u32[]{:S(2)}) copy-start(bf16[64,2048]{1,0:T(8,128)(2,1)} %resid.1) | copy-start | bytes 786436
  16.1 19.6 %copy-start.4 = (bf16[128,512]{1,0:T(8,128)(2,1)S(1)}, bf16[128,512]{1,0:T(8,128)(2,1)}, u32[]{:S(2)}) copy-start(bf16[128,512]{1,0:T(8,128)(2,1)} %sresid.1) | copy-start | bytes 393220
  35.7 1.2 copy-start.2
  121.8 4.2 %copy-start.5 = (bf16[512,4096]{1,0:T(8,128)(2,1)S(1)}, bf16[512,4096]{1,0:T(8,128)(2,1)}, u32[]{:S(2)}) copy-start(bf16[512,4096]{1,0:T(8,128)(2,1)} %get-tuple-element.8) | copy-start | bytes 12582916
Sparse Core Ops, SparseCore 0:
  17.7 18.0 all-gather.1

commit v3 on v2

v3 whole, which is shorter than its diff:
```python
import functools

import jax
import jax.numpy as jnp
from jax import lax
from jax.experimental import pallas as pl
from jax.experimental.pallas import tpu as pltpu
from jax.sharding import PartitionSpec as P

HEADS = 64
KV_HEADS = 8
HEAD = 128
PIECES = 4
EPS = 1e-05
MESH = pl.DeviceIdType.MESH
F32 = jnp.float32
BF16 = jnp.bfloat16


def position_of(index, n):
    z, x = index // 2, index % 2
    return z + x * (n - 1 - 2 * z)


def index_at(position, n):
    side = position // (n // 2)
    return 2 * (position + side * (n - 1 - 2 * position)) + side


class Gather:
    def __init__(self, block, mine, mn, mp, sends, recvs, passes, own=None):
        self.block, self.mine, self.mn, self.mp, self.own = block, mine, mn, mp, own
        self.sends, self.recvs, self.passes = sends, recvs, passes
        self.core, self.group, self.groups = mp % 2, mp // 2, mn // 2
        self.sibling = self.group * 2 + (1 - self.core)

    def same(self, j):
        return ((self.group + j) % self.groups) * 2 + self.core

    def other(self, j):
        return ((self.group + j) % self.groups) * 2 + (1 - self.core)

    def copy(self, source, who, send_sem, target):
        return pltpu.make_async_remote_copy(
            src_ref=source,
            dst_ref=self.block(who),
            send_sem=send_sem,
            recv_sem=self.recvs.at[who],
            device_id={"mp": target},
            device_id_type=MESH,
        )

    def first(self, j):
        target = self.same(j) if j else self.sibling
        return self.copy(self.mine, self.mp, self.sends.at[j], target)

    def start(self):
        for j in range(self.groups):
            self.first(j).start()

    def passed(self, j):
        who = self.same(j)
        return self.copy(self.block(who), who, self.passes.at[j], self.sibling)

    def forward(self):
        for j in range(1, self.groups):
            self.passed(j).wait_recv()
            self.passed(j).start()

    def finish(self):
        for j in range(self.groups):
            who = self.other(j)
            self.copy(self.block(who), who, self.sends.at[j], self.sibling).wait_recv()
        for j in range(self.groups):
            self.first(j).wait_send()
        for j in range(1, self.groups):
            self.passed(j).wait_send()


def to_columns(row, rows, width):
    tile = jnp.transpose(jnp.broadcast_to(row, (128, rows)))
    return jnp.concatenate([tile] * (width // 128), axis=1) if width > 128 else tile


def sum_to_row(values):
    ones = jnp.ones((8, values.shape[1]), F32)
    return lax.dot_general(
        ones, values, (((1,), (1,)), ((), ())),
        precision=lax.Precision.HIGHEST, preferred_element_type=F32,
    )


def middle(
    n, mn, width, tokens,
    query, keys_hbm, values_hbm, tout_hbm, resid, proj_hbm, sctx_hbm, sresid, sout_hbm, gains,
    hid_out, sall_out, err_out, st_out, coef_out, gain_out,
    kv, ctx, tout, proj, sctx, sout, head, hid, rs, tsend, trecv, err, st, state, sq, inn, coef,
    load, store, rs_send, rs_recv, ag_send, ag_recv, t_send, t_recv,
    sq_send, sq_recv, in_send, in_recv, co_send, co_recv,
    k_send, k_recv, k_pass, c_send, c_recv, c_pass,
    s_send, s_recv, s_pass, st_send, st_recv, st_pass, e_send, e_recv, e_pass,
):
    d, m = lax.axis_index("dp"), lax.axis_index("mp")
    rows = tokens // mn
    shard = tokens // n
    half = shard // 2
    per = n // mn
    features, columns = proj.shape
    piece = features // PIECES
    heads = query.shape[1] // HEAD
    p = position_of(d, n)
    my_rows = pl.ds(pl.multiple_of(m * rows, rows), rows)

    kv_cols = pl.ds(pl.multiple_of((d * heads // (HEADS // KV_HEADS)) * HEAD, HEAD), HEAD)
    loads = [
        pltpu.make_async_copy(src, dst, load.at[i])
        for i, (src, dst) in enumerate(
            (
                (keys_hbm.at[:, kv_cols], kv.at[my_rows, 0:HEAD]),
                (values_hbm.at[:, kv_cols], kv.at[my_rows, HEAD : 2 * HEAD]),
                (sctx_hbm, sctx),
                (sout_hbm, sout),
                (tout_hbm, tout),
                (proj_hbm, proj),
            )
        )
    ]
    for one in loads:
        one.start()

    barrier = pltpu.get_barrier_semaphore()
    for j in range(1, n):
        pl.semaphore_signal(barrier, inc=1, device_id={"dp": (d + j) % n}, device_id_type=MESH)
    for j in range(1, mn):
        pl.semaphore_signal(barrier, inc=1, device_id={"mp": (m + j) % mn}, device_id_type=MESH)
    pl.semaphore_wait(barrier, n - 1 + mn - 1)

    def block_of(ref, cols=slice(None)):
        return lambda who: ref.at[pl.ds(pl.multiple_of(who * rows, rows), rows), cols]

    loads[0].wait()
    loads[1].wait()
    pair = Gather(block_of(kv), kv.at[my_rows, :], mn, m, k_send, k_recv, k_pass)
    pair.start()

    def exchange(buf, sends, recvs, j):
        return pltpu.make_async_remote_copy(
            src_ref=buf.at[d],
            dst_ref=buf.at[d],
            send_sem=sends.at[j],
            recv_sem=recvs.at[d],
            device_id={"dp": (d + j) % n},
            device_id_type=MESH,
        )

    def exchange_wait(buf, sends, recvs):
        for j in range(1, n):
            who = (d + j) % n
            pltpu.make_async_remote_copy(
                src_ref=buf.at[who], dst_ref=buf.at[who], send_sem=sends.at[j],
                recv_sem=recvs.at[who], device_id={"dp": who}, device_id_type=MESH,
            ).wait_recv()
        for j in range(1, n):
            exchange(buf, sends, recvs, j).wait_send()

    def total_of(buf):
        whole = buf[0]
        for j in range(1, n):
            whole = whole + buf[j]
        return whole

    loads[2].wait()
    loads[3].wait()
    state[...] = sresid[...].astype(F32) + jnp.dot(sctx[...], sout[...], preferred_element_type=F32)
    pair.forward()
    st[my_rows, :] = state[...].astype(BF16)
    sq[d] = sum_to_row(state[...] * state[...])
    gain = gains[:, pl.ds(pl.multiple_of(d * columns, columns), columns)]
    gain_out[...] = gain
    pair.finish()

    query_pos = m * rows + lax.broadcasted_iota(jnp.int32, (rows, tokens), 0)
    allowed = query_pos >= lax.broadcasted_iota(jnp.int32, (rows, tokens), 1)
    keys, values = kv[:, 0:HEAD], kv[:, HEAD : 2 * HEAD]
    contexts = []
    for part in range(2):
        for h in range(part * heads // 2, (part + 1) * heads // 2):
            cols = slice(h * HEAD, (h + 1) * HEAD)
            scores = lax.dot_general(
                query[:, cols], keys, (((1,), (1,)), ((), ())), preferred_element_type=F32
            ) * HEAD ** (-0.5)
            scores = jnp.where(allowed, scores, -jnp.inf)
            weights = jnp.exp(scores - jnp.max(scores, axis=1, keepdims=True))
            whole = jnp.sum(weights, axis=1, keepdims=True)
            mixed = jnp.dot(weights.astype(BF16), values, preferred_element_type=F32)
            ctx[my_rows, cols] = (mixed / whole).astype(BF16)
        cols = slice(part * heads // 2 * HEAD, (part + 1) * heads // 2 * HEAD)
        contexts.append(
            Gather(
                block_of(ctx, cols), ctx.at[my_rows, cols], mn, m,
                c_send.at[part], c_recv.at[part], c_pass.at[part],
            )
        )
        contexts[part].start()
    for part in range(2):
        contexts[part].forward()
    for j in range(1, n):
        exchange(sq, sq_send, sq_recv, j).start()
    student = Gather(block_of(sall_out), sctx_hbm, mn, m, s_send, s_recv, s_pass)
    student.start()
    keep = pltpu.make_async_copy(sctx_hbm, sall_out.at[my_rows, :], store.at[0])
    keep.start()
    states = Gather(block_of(st), st.at[my_rows, :], mn, m, st_send, st_recv, st_pass)
    states.start()
    loads[4].wait()
    for part in range(2):
        contexts[part].finish()

    def chunk(position, way):
        start = index_at(position, n) * shard + way * half
        return pl.ds(pl.multiple_of(start, half), half)

    def toward(way):
        return index_at((p + 1 - 2 * way + n) % n, n)

    def at(way, s):
        return (p - (1 - 2 * way) * s + 2 * n) % n

    def cut(k):
        return slice(k * piece, (k + 1) * piece)

    def reduce_copy(s, way, k):
        return pltpu.make_async_remote_copy(
            src_ref=head.at[chunk(at(way, s + 1), way), cut(k)],
            dst_ref=rs.at[way, s, k],
            send_sem=rs_send.at[way, s, k],
            recv_sem=rs_recv.at[way, s, k],
            device_id={"dp": toward(way)},
            device_id_type=MESH,
        )

    for k in range(PIECES):
        head[:, cut(k)] = jnp.dot(
            ctx[...], tout[:, cut(k)], preferred_element_type=F32
        ).astype(BF16)
        for way in (0, 1):
            reduce_copy(0, way, k).start()

    @pl.loop(1, n - 1)
    def _(s):
        for k in range(PIECES):
            for way in (0, 1):
                where = chunk(at(way, s + 1), way)
                reduce_copy(s - 1, way, k).wait_recv()
                summed = head[where, cut(k)].astype(F32) + rs[way, s - 1, k].astype(F32)
                head[where, cut(k)] = summed.astype(BF16)
                reduce_copy(s, way, k).start()

    def moving(s, way, k, where):
        return pltpu.make_async_remote_copy(
            src_ref=hid.at[where, cut(k)],
            dst_ref=hid.at[where, cut(k)],
            send_sem=ag_send.at[way, s, k],
            recv_sem=ag_recv.at[way, s, k],
            device_id={"dp": toward(way)},
            device_id_type=MESH,
        )

    def gather_copy(s, way, k):
        return moving(s, way, k, chunk(at(way, s), way))

    def arrival(s, way, k):
        return moving(s, way, k, chunk(at(way, s + 1), way))

    for k in range(PIECES):
        for way in (0, 1):
            reduce_copy(n - 2, way, k).wait_recv()
            where = chunk(p, way)
            mine = pl.ds(way * half, half)
            summed = head[where, cut(k)].astype(F32) + rs[way, n - 2, k].astype(F32)
            hid[where, cut(k)] = (resid[mine, cut(k)].astype(F32) + summed).astype(BF16)
            gather_copy(0, way, k).start()

    def target_copy(owner, way):
        to = owner // per
        place = pl.ds(pl.multiple_of((owner % per) * shard + way * half, half), half)
        start = pl.ds(pl.multiple_of(owner * shard + way * half, half), half)
        return pltpu.make_async_remote_copy(
            src_ref=tsend.at[start, :],
            dst_ref=trecv.at[m, place, :],
            send_sem=t_send.at[way, owner],
            recv_sem=t_recv.at[m, way, owner % per],
            device_id={"mp": to},
            device_id_type=MESH,
        )

    def project(s, arrive, forward):
        where = [chunk(at(way, s), way) for way in (0, 1)]
        out = None
        for k in range(PIECES):
            for way in (0, 1):
                if arrive:
                    arrival(s - 1, way, k).wait_recv()
                if forward:
                    gather_copy(s, way, k).start()
            both = jnp.concatenate([hid[w, cut(k)] for w in where], axis=0)
            term = jnp.dot(both, proj[cut(k), :], preferred_element_type=F32)
            out = term if out is None else out + term
        out = out.astype(BF16)
        for way in (0, 1):
            tsend[where[way], :] = out[way * half : (way + 1) * half]
            owner = index_at(at(way, s), n)

            @pl.when(owner // per != m)
            def _():
                target_copy(owner, way).start()

    loads[5].wait()
    project(0, False, False)

    @pl.loop(1, n - 1)
    def _(s):
        project(s, True, True)

    project(n - 1, True, False)
    hid_store = pltpu.make_async_copy(hid, hid_out, store.at[1])
    hid_store.start()
    states.forward()
    student.forward()

    exchange_wait(sq, sq_send, sq_recv)
    inverse_row = lax.rsqrt(total_of(sq) / width + EPS)
    inverse = to_columns(inverse_row[0:1], rows, columns)
    pred = state[...] * inverse * gain

    target = tsend[my_rows, :].astype(F32)
    for j in range(1, mn):
        who = (m + j) % mn
        for way in (0, 1):
            for k in range(per):
                place = pl.ds(k * shard + way * half, half)
                pltpu.make_async_remote_copy(
                    src_ref=trecv.at[who, place, :],
                    dst_ref=trecv.at[who, place, :],
                    send_sem=t_send.at[way, k],
                    recv_sem=t_recv.at[who, way, k],
                    device_id={"mp": who},
                    device_id_type=MESH,
                ).wait_recv()
        target = target + trecv[who].astype(F32)

    error = (pred - target) * (tokens ** -0.5)
    err[my_rows, :] = error.astype(BF16)
    errors = Gather(block_of(err), err.at[my_rows, :], mn, m, e_send, e_recv, e_pass)
    errors.start()
    inn[d] = sum_to_row(error * gain * state[...])
    for j in range(1, n):
        exchange(inn, in_send, in_recv, j).start()

    states.finish()
    st_store = pltpu.make_async_copy(st, st_out, store.at[2])
    st_store.start()

    exchange_wait(inn, in_send, in_recv)
    inner_row = total_of(inn)
    coef[m, 0:8, :] = inverse_row
    coef[m, 8:16, :] = inverse_row * inverse_row * inverse_row * (inner_row / width)

    def coef_copy(j):
        return pltpu.make_async_remote_copy(
            src_ref=coef.at[m], dst_ref=coef.at[m], send_sem=co_send.at[j],
            recv_sem=co_recv.at[m], device_id={"mp": (m + j) % mn}, device_id_type=MESH,
        )

    for j in range(1, mn):
        coef_copy(j).start()
    errors.forward()
    student.finish()
    errors.finish()
    err_store = pltpu.make_async_copy(err, err_out, store.at[3])
    err_store.start()
    for j in range(1, mn):
        who = (m + j) % mn
        pltpu.make_async_remote_copy(
            src_ref=coef.at[who], dst_ref=coef.at[who], send_sem=co_send.at[j],
            recv_sem=co_recv.at[who], device_id={"mp": who}, device_id_type=MESH,
        ).wait_recv()
    for j in range(1, mn):
        coef_copy(j).wait_send()
    coef_out[...] = coef[...]

    @pl.loop(0, n - 1)
    def _(s):
        for way in (0, 1):
            for k in range(PIECES):
                reduce_copy(s, way, k).wait_send()
                gather_copy(s, way, k).wait_send()

    @pl.loop(0, n)
    def _(owner):
        @pl.when(owner // per != m)
        def _():
            for way in (0, 1):
                target_copy(owner, way).wait_send()

    keep.wait()
    hid_store.wait()
    st_store.wait()
    err_store.wait()


def on_device(
    n,
    mn,
    teacher_query,
    teacher_keys,
    teacher_values,
    teacher_out,
    teacher_resid,
    distill_proj,
    student_context,
    student_resid,
    student_out,
    student_gain,
):
    features, columns = distill_proj.shape
    width = student_context.shape[1]
    rows = teacher_query.shape[0]
    total = rows * mn
    shard = total // n
    vmem = pl.BlockSpec(memory_space=pltpu.VMEM)
    anywhere = pl.BlockSpec(memory_space=pl.ANY)
    dma = pltpu.SemaphoreType.DMA
    pairs = mn // 2
    hidden, student_all, error, state, coef, gain = pl.pallas_call(
        functools.partial(middle, n, mn, width, total),
        out_shape=(
            jax.ShapeDtypeStruct((total, features), BF16),
            jax.ShapeDtypeStruct((total, width), BF16),
            jax.ShapeDtypeStruct((total, columns), BF16),
            jax.ShapeDtypeStruct((total, columns), BF16),
            jax.ShapeDtypeStruct((mn, 16, rows), F32),
            jax.ShapeDtypeStruct((1, columns), F32),
        ),
        in_specs=[
            vmem, anywhere, anywhere, anywhere, vmem, anywhere, anywhere, vmem, anywhere, vmem,
        ],
        out_specs=(anywhere, anywhere, anywhere, anywhere, vmem, vmem),
        scratch_shapes=[
            pltpu.VMEM((total, 2 * HEAD), BF16),
            pltpu.VMEM((total, teacher_query.shape[1]), BF16),
            pltpu.VMEM(teacher_out.shape, BF16),
            pltpu.VMEM(distill_proj.shape, BF16),
            pltpu.VMEM(student_context.shape, BF16),
            pltpu.VMEM(student_out.shape, BF16),
            pltpu.VMEM((total, features), BF16),
            pltpu.VMEM((total, features), BF16),
            pltpu.VMEM((2, n - 1, PIECES, shard // 2, features // PIECES), BF16),
            pltpu.VMEM((total, columns), BF16),
            pltpu.VMEM((mn, rows, columns), BF16),
            pltpu.VMEM((total, columns), BF16),
            pltpu.VMEM((total, columns), BF16),
            pltpu.VMEM((rows, columns), F32),
            pltpu.VMEM((n, 8, rows), F32),
            pltpu.VMEM((n, 8, rows), F32),
            pltpu.VMEM((mn, 16, rows), F32),
            dma((6,)),
            dma((4,)),
            dma((2, n - 1, PIECES)),
            dma((2, n - 1, PIECES)),
            dma((2, n - 1, PIECES)),
            dma((2, n - 1, PIECES)),
            dma((2, n)),
            dma((mn, 2, n // mn)),
            dma((n,)), dma((n,)), dma((n,)), dma((n,)),
            dma((mn,)), dma((mn,)),
            dma((pairs,)), dma((mn,)), dma((pairs,)),
            dma((2, pairs)), dma((2, mn)), dma((2, pairs)),
            dma((pairs,)), dma((mn,)), dma((pairs,)),
            dma((pairs,)), dma((mn,)), dma((pairs,)),
            dma((pairs,)), dma((mn,)), dma((pairs,)),
        ],
        compiler_params=pltpu.CompilerParams(
            collective_id=0, has_side_effects=True, vmem_limit_bytes=48 * 1024 * 1024
        ),
        name="middle",
    )(
        teacher_query, teacher_keys, teacher_values, teacher_out, teacher_resid, distill_proj,
        student_context, student_resid, student_out, student_gain.reshape(1, width),
    )
    inverse = coef[:, 0, :].reshape(total, 1)
    pull = coef[:, 8, :].reshape(total, 1)
    wide = error.astype(F32) * inverse
    kept = state.astype(F32)
    grad_gain = jnp.sum(wide * kept, axis=0)
    grad_state = (wide * gain - kept * pull).astype(BF16)
    contract_rows = (((0,), (0,)), ((), ()))
    grad_proj = -lax.dot_general(hidden, error, contract_rows, preferred_element_type=F32)
    grad_wo = lax.dot_general(
        student_all, grad_state, contract_rows, preferred_element_type=F32
    ).astype(BF16)
    return (grad_wo, grad_gain, grad_proj)


def solution(mesh):
    in_specs = (
        P("mp", "dp"),
        P("mp", None),
        P("mp", None),
        P("dp", "mp"),
        P("dp", "mp"),
        P("mp", "dp"),
        P("mp", None),
        P("mp", "dp"),
        P(None, "dp"),
        P(),
    )
    out_specs = (P(None, "dp"), P("dp"), P("mp", "dp"))
    return jax.shard_map(
        functools.partial(on_device, mesh.shape["dp"], mesh.shape["mp"]),
        mesh=mesh, in_specs=in_specs, out_specs=out_specs, check_vma=False,
    )
```

time: 138 us -> 99.8 us (0.72)
  waiting for transfers between devices: 17.4 us -> 0 us
  between operations: 14.2 us -> 0.67 us
  blocking collectives: 7.22 us -> 0 us
  Pallas kernels: 84.8 us -> 81.2 us
  local copies, waits for them, and re-layouts: 3.66 us -> 6.64 us
    all_gather x1 -> x0, waiting for transfers between devices: 17.4 us -> none  [on_device(): context_all = lax.all_gather(context, 'mp', axis=0, tiled=True)]
    all_gather x1 -> x0, blocking collectives: 7.22 us -> none  [on_device(): lax.all_gather(jnp.concatenate([key_mine, value_mine], 1), 'mp', axis=0,...]
    unnamed x12 -> x14, local copies, waits for them, and re-layouts: 1.26 us -> 6.64 us
    pallas_call x1, Pallas kernels: 84.8 us -> 81.2 us  [on_device(): pl.pallas_call(functools.partial(middle, n, mn, width, total), out_shape=...]
    dot_general x1, matrix products: 4.62 us -> 6.73 us  [on_device(): lax.dot_general(student_all, grad_state, contract_rows, preferred_element...]
    dynamic_slice x2 -> x0, local copies, waits for them, and re-layouts: 1.55 us -> none  [the longest x1 0.79 us: on_device(): lax.dynamic_slice_in_dim(teacher_values, kv_start * HEAD, kv_local * HEAD...]
  transfers between devices with their start and end apart: 1 -> 0, of which waited for: 1 -> 0; matrix products, arithmetic and copies ran while one was open for 1% -> 0% of each run, Pallas kernels for 0% -> 0%
where the time goes in v3:
time: 99.8 us; the launch traced here: 99.4 us
  Pallas kernels  81.2 us (81%)
  matrix products  10 us (10%)
  local copies, waits for them, and re-layouts  6.64 us (7%)
    pallas_call x1, Pallas kernels, on_device(): pl.pallas_call(functools.partial(middle, n, mn, width, total), out_shape=...  81.2 us
    dot_general x1, matrix products, on_device(): lax.dot_general(student_all, grad_state, contract_rows, preferred_element...  6.73 us
    unnamed x14, local copies, waits for them, and re-layouts  6.64 us
    dot_general x1, matrix products, on_device(): lax.dot_general(hidden, error, contract_rows, preferred_element_type=F32)  3.31 us

profile of v3, /device:TPU:0, one launch (start us, length us, event | category | flops | bytes accessed | tf_op | source)
XLA Modules:
  0.0 99.4 jit_solution(1157503495518398037)
XLA Ops:
  0.6 0.0 copy-start
  0.6 1.2 %copy-done = bf16[128,4096]{1,0:T(8,128)(2,1)S(1)} copy-done((bf16[128,4096]{1,0:T(8,128)(2,1)S(1)}, bf16[128,4096]{1,0:T(8,128)(2,1)}, u32[]{:S(2)}) %copy-start) | copy-done | bytes 1048600
  1.9 0.0 copy-start.1
  1.9 0.9 copy-done.1
  2.8 0.0 copy-start.2
  2.8 0.9 copy-done.2
  3.8 0.0 copy-start.3
  3.8 0.9 copy-done.3
  4.7 0.0 copy-start.4
  4.7 0.9 copy-done.4
  5.7 0.0 copy-start.5
  5.7 0.9 copy-done.5
  6.6 0.0 copy-start.6
  6.6 0.7 copy-done.6
  7.3 81.2 %middle.1 = (bf16[512,2048]{1,0:T(8,128)(2,1)S(1)}, bf16[512,4096]{1,0:T(8,128)(2,1)}, bf16[512,512]{1,0:T(8,128)(2,1)S(1)}, bf16[512,512]{1,0:T(8,128)(2,1)S(1)...) custom-call(bf16[128,1024]{1,0:T(8,128)(2,1)S(1)} %copy-done.1, bf16[128,1024]{1,0:T(8,128)(2,1)S(1)} %copy-done.2, ...), custom_call_target="tpu_custom_call" | custom-call | tf_op jit(solution)/shard_map/middle/pallas_call | solution.py:435
  88.5 6.7 %convolution_convert_fusion = bf16[4096,512]{1,0:T(8,128)(2,1)} fusion(bf16[512,4096]{1,0:T(8,128)(2,1)} %get-tuple-element.9, bf16[512,512]{1,0:T(8,128)(2,1)S(1)} %get-tuple-element.13, bf16[512,512]{1,0:T(8,128)(2,1)S(1)} %get-tuple-element.10, f32[512]{0:T(512)S(1)} %bitcast.11, f32[512]{0:T(512)S(1)} %bitcast.8, f32[512]{0:T(512)S(1)} %bitcast.9), kind=kOutput, calls=%fused_computation | convolution fusion | flops 2151415808 | bytes 9443328 | tf_op jit(solution)/shard_map/dot_general | solution.py:499
  95.2 0.8 fusion.2
  96.1 3.3 %convolution_negate_fusion = f32[2048,512]{1,0:T(8,128)} fusion(bf16[512,2048]{1,0:T(8,128)(2,1)S(1)} %get-tuple-element.14, bf16[512,512]{1,0:T(8,128)(2,1)S(1)} %get-tuple-element.10), kind=kOutput, calls=%fused_computation.1 | convolution fusion | flops 1074790400 | bytes 6815744 | tf_op jit(solution)/shard_map/dot_general | solution.py:498
  (1 shorter events, 0.0 us)
Async XLA Ops:
  0.6 1.2 %copy-start = (bf16[128,4096]{1,0:T(8,128)(2,1)S(1)}, bf16[128,4096]{1,0:T(8,128)(2,1)}, u32[]{:S(2)}) copy-start(bf16[128,4096]{1,0:T(8,128)(2,1)} %sctx_hbm.1) | copy-start | bytes 3145732
  1.9 0.9 copy-start.1
  2.8 0.9 copy-start.2
  3.8 0.9 copy-start.3
  4.7 0.9 copy-start.4
  5.7 0.9 copy-start.5
  6.6 0.7 copy-start.6

commit v4 on v3

--- a/solution.py
+++ b/solution.py
@@ -11,6 +11,8 @@
 KV_HEADS = 8
 HEAD = 128
 PIECES = 4
+STEPS = 4
+VMEM_BYTES = 56 * 1024 * 1024
 EPS = 1e-05
 MESH = pl.DeviceIdType.MESH
 F32 = jnp.float32
@@ -92,9 +94,11 @@
 
 def middle(
     n, mn, width, tokens,
-    query, keys_hbm, values_hbm, tout_hbm, resid, proj_hbm, sctx_hbm, sresid, sout_hbm, gains,
-    hid_out, sall_out, err_out, st_out, coef_out, gain_out,
-    kv, ctx, tout, proj, sctx, sout, head, hid, rs, tsend, trecv, err, st, state, sq, inn, coef,
+    query_hbm, keys_hbm, values_hbm, tout_hbm, resid_hbm, proj_hbm, sctx_hbm, sresid_hbm, sout_hbm,
+    gain_hbm,
+    hid_out, sall, err_out, st_out, coef_out, gain_out,
+    hid, err, st, coef, gain_ref, sctx, query, resid, sresid,
+    kv, ctx, tout, proj, sout, head, rs, tsend, trecv, state, sq, inn,
     load, store, rs_send, rs_recv, ag_send, ag_recv, t_send, t_recv,
     sq_send, sq_recv, in_send, in_recv, co_send, co_recv,
     k_send, k_recv, k_pass, c_send, c_recv, c_pass,
@@ -112,6 +116,7 @@
     my_rows = pl.ds(pl.multiple_of(m * rows, rows), rows)
 
     kv_cols = pl.ds(pl.multiple_of((d * heads // (HEADS // KV_HEADS)) * HEAD, HEAD), HEAD)
+    gain_cols = pl.ds(pl.multiple_of(d * columns, columns), columns)
     loads = [
         pltpu.make_async_copy(src, dst, load.at[i])
         for i, (src, dst) in enumerate(
@@ -122,6 +127,10 @@
                 (sout_hbm, sout),
                 (tout_hbm, tout),
                 (proj_hbm, proj),
+                (query_hbm, query),
+                (resid_hbm, resid),
+                (sresid_hbm, sresid),
+                (gain_hbm.at[:, gain_cols], gain_ref),
             )
         )
     ]
@@ -171,13 +180,15 @@
 
     loads[2].wait()
     loads[3].wait()
+    loads[8].wait()
+    loads[9].wait()
     state[...] = sresid[...].astype(F32) + jnp.dot(sctx[...], sout[...], preferred_element_type=F32)
     pair.forward()
     st[my_rows, :] = state[...].astype(BF16)
     sq[d] = sum_to_row(state[...] * state[...])
-    gain = gains[:, pl.ds(pl.multiple_of(d * columns, columns), columns)]
-    gain_out[...] = gain
+    gain = gain_ref[...]
     pair.finish()
+    loads[6].wait()
 
     query_pos = m * rows + lax.broadcasted_iota(jnp.int32, (rows, tokens), 0)
     allowed = query_pos >= lax.broadcasted_iota(jnp.int32, (rows, tokens), 1)
@@ -206,10 +217,23 @@
         contexts[part].forward()
     for j in range(1, n):
         exchange(sq, sq_send, sq_recv, j).start()
-    student = Gather(block_of(sall_out), sctx_hbm, mn, m, s_send, s_recv, s_pass)
+    student = Gather(block_of(sall), sctx, mn, m, s_send, s_recv, s_pass)
     student.start()
-    keep = pltpu.make_async_copy(sctx_hbm, sall_out.at[my_rows, :], store.at[0])
-    keep.start()
+    stores = [
+        pltpu.make_async_copy(src, dst, store.at[i])
+        for i, (src, dst) in enumerate(
+            (
+                (sctx, sall.at[my_rows, :]),
+                (gain_ref, gain_out),
+                (hid, hid_out),
+                (st, st_out),
+                (err, err_out),
+                (coef, coef_out),
+            )
+        )
+    ]
+    stores[0].start()
+    stores[1].start()
     states = Gather(block_of(st), st.at[my_rows, :], mn, m, st_send, st_recv, st_pass)
     states.start()
     loads[4].wait()
@@ -272,6 +296,7 @@
     def arrival(s, way, k):
         return moving(s, way, k, chunk(at(way, s + 1), way))
 
+    loads[7].wait()
     for k in range(PIECES):
         for way in (0, 1):
             reduce_copy(n - 2, way, k).wait_recv()
@@ -323,8 +348,7 @@
         project(s, True, True)
 
     project(n - 1, True, False)
-    hid_store = pltpu.make_async_copy(hid, hid_out, store.at[1])
-    hid_store.start()
+    stores[2].start()
     states.forward()
     student.forward()
 
@@ -358,8 +382,7 @@
         exchange(inn, in_send, in_recv, j).start()
 
     states.finish()
-    st_store = pltpu.make_async_copy(st, st_out, store.at[2])
-    st_store.start()
+    stores[3].start()
 
     exchange_wait(inn, in_send, in_recv)
     inner_row = total_of(inn)
@@ -377,17 +400,16 @@
     errors.forward()
     student.finish()
     errors.finish()
-    err_store = pltpu.make_async_copy(err, err_out, store.at[3])
-    err_store.start()
+    stores[4].start()
     for j in range(1, mn):
         who = (m + j) % mn
         pltpu.make_async_remote_copy(
             src_ref=coef.at[who], dst_ref=coef.at[who], send_sem=co_send.at[j],
             recv_sem=co_recv.at[who], device_id={"mp": who}, device_id_type=MESH,
         ).wait_recv()
+    stores[5].start()
     for j in range(1, mn):
         coef_copy(j).wait_send()
-    coef_out[...] = coef[...]
 
     @pl.loop(0, n - 1)
     def _(s):
@@ -403,10 +425,34 @@
             for way in (0, 1):
                 target_copy(owner, way).wait_send()
 
-    keep.wait()
-    hid_store.wait()
-    st_store.wait()
-    err_store.wait()
+    for one in stores:
+        one.wait()
+
+
+def finish(hid, sall, err, st, coef, gain, grad_wo, grad_gain, grad_proj, grad_state):
+    i = pl.program_id(0)
+    tokens, columns = err.shape
+    rows = coef.shape[2]
+
+    @pl.when(i == 0)
+    def _():
+        total = jnp.zeros((1, columns), F32)
+        for block in range(tokens // rows):
+            where = slice(block * rows, (block + 1) * rows)
+            wide = err[where, :].astype(F32) * to_columns(coef[block, 0:1], rows, columns)
+            kept = st[where, :].astype(F32)
+            pull = to_columns(coef[block, 8:9], rows, columns)
+            total = total + jnp.sum(wide * kept, axis=0, keepdims=True)
+            grad_state[where, :] = (wide * gain[...] - kept * pull).astype(BF16)
+        grad_gain[...] = total
+
+    def part(left, right):
+        return lax.dot_general(
+            left[...], right[...], (((0,), (0,)), ((), ())), preferred_element_type=F32
+        )
+
+    grad_proj[...] = -part(hid, err)
+    grad_wo[...] = part(sall, grad_state).astype(BF16)
 
 
 def on_device(
@@ -429,10 +475,9 @@
     total = rows * mn
     shard = total // n
     vmem = pl.BlockSpec(memory_space=pltpu.VMEM)
-    anywhere = pl.BlockSpec(memory_space=pl.ANY)
     dma = pltpu.SemaphoreType.DMA
     pairs = mn // 2
-    hidden, student_all, error, state, coef, gain = pl.pallas_call(
+    gathered = pl.pallas_call(
         functools.partial(middle, n, mn, width, total),
         out_shape=(
             jax.ShapeDtypeStruct((total, features), BF16),
@@ -442,30 +487,32 @@
             jax.ShapeDtypeStruct((mn, 16, rows), F32),
             jax.ShapeDtypeStruct((1, columns), F32),
         ),
-        in_specs=[
-            vmem, anywhere, anywhere, anywhere, vmem, anywhere, anywhere, vmem, anywhere, vmem,
-        ],
-        out_specs=(anywhere, anywhere, anywhere, anywhere, vmem, vmem),
+        in_specs=[pl.BlockSpec(memory_space=pltpu.HBM)] * 10,
+        out_specs=[pl.BlockSpec(memory_space=pltpu.HBM)] * 6,
         scratch_shapes=[
+            pltpu.VMEM((total, features), BF16),
+            pltpu.VMEM((total, columns), BF16),
+            pltpu.VMEM((total, columns), BF16),
+            pltpu.VMEM((mn, 16, rows), F32),
+            pltpu.VMEM((1, columns), F32),
+            pltpu.VMEM(student_context.shape, BF16),
+            pltpu.VMEM(teacher_query.shape, BF16),
+            pltpu.VMEM(teacher_resid.shape, BF16),
+            pltpu.VMEM(student_resid.shape, BF16),
             pltpu.VMEM((total, 2 * HEAD), BF16),
             pltpu.VMEM((total, teacher_query.shape[1]), BF16),
             pltpu.VMEM(teacher_out.shape, BF16),
             pltpu.VMEM(distill_proj.shape, BF16),
-            pltpu.VMEM(student_context.shape, BF16),
             pltpu.VMEM(student_out.shape, BF16),
-            pltpu.VMEM((total, features), BF16),
             pltpu.VMEM((total, features), BF16),
             pltpu.VMEM((2, n - 1, PIECES, shard // 2, features // PIECES), BF16),
             pltpu.VMEM((total, columns), BF16),
             pltpu.VMEM((mn, rows, columns), BF16),
-            pltpu.VMEM((total, columns), BF16),
-            pltpu.VMEM((total, columns), BF16),
             pltpu.VMEM((rows, columns), F32),
             pltpu.VMEM((n, 8, rows), F32),
             pltpu.VMEM((n, 8, rows), F32),
-            pltpu.VMEM((mn, 16, rows), F32),
+            dma((10,)),
             dma((6,)),
-            dma((4,)),
             dma((2, n - 1, PIECES)),
             dma((2, n - 1, PIECES)),
             dma((2, n - 1, PIECES)),
@@ -481,25 +528,37 @@
             dma((pairs,)), dma((mn,)), dma((pairs,)),
         ],
         compiler_params=pltpu.CompilerParams(
-            collective_id=0, has_side_effects=True, vmem_limit_bytes=48 * 1024 * 1024
+            collective_id=0, has_side_effects=True, vmem_limit_bytes=VMEM_BYTES
         ),
         name="middle",
     )(
         teacher_query, teacher_keys, teacher_values, teacher_out, teacher_resid, distill_proj,
         student_context, student_resid, student_out, student_gain.reshape(1, width),
     )
-    inverse = coef[:, 0, :].reshape(total, 1)
-    pull = coef[:, 8, :].reshape(total, 1)
-    wide = error.astype(F32) * inverse
-    kept = state.astype(F32)
-    grad_gain = jnp.sum(wide * kept, axis=0)
-    grad_state = (wide * gain - kept * pull).astype(BF16)
-    contract_rows = (((0,), (0,)), ((), ()))
-    grad_proj = -lax.dot_general(hidden, error, contract_rows, preferred_element_type=F32)
-    grad_wo = lax.dot_general(
-        student_all, grad_state, contract_rows, preferred_element_type=F32
-    ).astype(BF16)
-    return (grad_wo, grad_gain, grad_proj)
+    steps = STEPS
+    grad_wo, grad_gain, grad_proj = pl.pallas_call(
+        finish,
+        grid=(steps,),
+        out_shape=(
+            jax.ShapeDtypeStruct((width, columns), BF16),
+            jax.ShapeDtypeStruct((1, columns), F32),
+            jax.ShapeDtypeStruct((features, columns), F32),
+        ),
+        in_specs=[
+            pl.BlockSpec((total, features // steps), lambda i: (0, i)),
+            pl.BlockSpec((total, width // steps), lambda i: (0, i)),
+            vmem, vmem, vmem, vmem,
+        ],
+        out_specs=(
+            pl.BlockSpec((width // steps, columns), lambda i: (i, 0)),
+            pl.BlockSpec((1, columns), lambda i: (0, 0)),
+            pl.BlockSpec((features // steps, columns), lambda i: (i, 0)),
+        ),
+        scratch_shapes=[pltpu.VMEM((total, columns), BF16)],
+        compiler_params=pltpu.CompilerParams(vmem_limit_bytes=VMEM_BYTES),
+        name="finish",
+    )(*gathered)
+    return (grad_wo, grad_gain.reshape(columns), grad_proj)
 
 
 def solution(mesh):

time: 99.8 us -> 91.1 us (0.913)
  matrix products: 10 us -> 0 us
  Pallas kernels: 81.2 us -> 90.3 us
  local copies, waits for them, and re-layouts: 6.64 us -> 0 us
    dot_general x2 -> x0, matrix products: 10 us -> none  [the longest x1 6.73 us: on_device(): lax.dot_general(student_all, grad_state, contract_rows, preferred_element...]
    pallas_call x0 -> x1, Pallas kernels: none -> 8.69 us  [on_device(): pl.pallas_call(finish, grid=(steps,), out_shape=(jax.ShapeDtypeStruct((wi...]
    unnamed x14 -> x0, local copies, waits for them, and re-layouts: 6.64 us -> none
where the time goes in v4:
time: 91.1 us; the launch traced here: 91 us
  Pallas kernels  90.3 us (99%)
    pallas_call x1, Pallas kernels, on_device(): pl.pallas_call(functools.partial(middle, n, mn, width, total), out_shape=...  81.6 us
    pallas_call x1, Pallas kernels, on_device(): pl.pallas_call(finish, grid=(steps,), out_shape=(jax.ShapeDtypeStruct((wi...  8.69 us

profile of v4, /device:TPU:0, one launch (start us, length us, event | category | flops | bytes accessed | tf_op | source)
XLA Modules:
  0.0 91.0 jit_solution(10195679419478346374)
XLA Ops:
  0.6 81.6 %middle.1 = (bf16[512,2048]{1,0:T(8,128)(2,1)}, bf16[512,4096]{1,0:T(8,128)(2,1)}, bf16[512,512]{1,0:T(8,128)(2,1)}, bf16[512,512]{1,0:T(8,128)(2,1)}, f32[4,16,128]{2,1,0:T(8,128)}, /*index=5*/f32[1,512]{1,0:T(1,128)}) custom-call(bf16[128,1024]{1,0:T(8,128)(2,1)} %query_hbm.1, bf16[128,1024]{1,0:T(8,128)(2,1)} %keys_hbm.1, bf16[128,1024]{1,0:T(8,128)(2,1)} %values_hbm.1, ...), custom_call_target="tpu_custom_call" | custom-call | tf_op jit(solution)/shard_map/middle/pallas_call | solution.py:480
  82.3 8.7 %finish.1 = (bf16[4096,512]{1,0:T(8,128)(2,1)}, f32[1,512]{1,0:T(1,128)}, f32[2048,512]{1,0:T(8,128)}) custom-call(bf16[512,2048]{1,0:T(8,128)(2,1)} %get-tuple-element.12.hid, bf16[512,4096]{1,0:T(8,128)(2,1)} %get-tuple-element.13.sall, bf16[512,512]{1,0:T(8,128)(2,1)} %get-tuple-element.14.err, bf16[512,512]{1,0:T(8,128)(2,1)} %get-tuple-element.15.st, ...), custom_call_target="tpu_custom_call" | custom-call | tf_op jit(solution)/shard_map/finish/pallas_call | solution.py:539

commit v5 on v4

--- a/solution.py
+++ b/solution.py
@@ -11,7 +11,8 @@
 KV_HEADS = 8
 HEAD = 128
 PIECES = 4
-STEPS = 4
+PARTS = 4
+STEPS = 8
 VMEM_BYTES = 56 * 1024 * 1024
 EPS = 1e-05
 MESH = pl.DeviceIdType.MESH
@@ -134,8 +135,9 @@
             )
         )
     ]
-    for one in loads:
-        one.start()
+    early = (0, 1, 6)
+    for i in early:
+        loads[i].start()
 
     barrier = pltpu.get_barrier_semaphore()
     for j in range(1, n):
@@ -151,6 +153,8 @@
     loads[1].wait()
     pair = Gather(block_of(kv), kv.at[my_rows, :], mn, m, k_send, k_recv, k_pass)
     pair.start()
+    for i in (2, 3, 4, 5, 7, 8, 9):
+        loads[i].start()
 
     def exchange(buf, sends, recvs, j):
         return pltpu.make_async_remote_copy(
@@ -178,15 +182,7 @@
             whole = whole + buf[j]
         return whole
 
-    loads[2].wait()
-    loads[3].wait()
-    loads[8].wait()
-    loads[9].wait()
-    state[...] = sresid[...].astype(F32) + jnp.dot(sctx[...], sout[...], preferred_element_type=F32)
     pair.forward()
-    st[my_rows, :] = state[...].astype(BF16)
-    sq[d] = sum_to_row(state[...] * state[...])
-    gain = gain_ref[...]
     pair.finish()
     loads[6].wait()
 
@@ -194,8 +190,9 @@
     allowed = query_pos >= lax.broadcasted_iota(jnp.int32, (rows, tokens), 1)
     keys, values = kv[:, 0:HEAD], kv[:, HEAD : 2 * HEAD]
     contexts = []
-    for part in range(2):
-        for h in range(part * heads // 2, (part + 1) * heads // 2):
+    parts = min(PARTS, heads)
+    for part in range(parts):
+        for h in range(part * heads // parts, (part + 1) * heads // parts):
             cols = slice(h * HEAD, (h + 1) * HEAD)
             scores = lax.dot_general(
                 query[:, cols], keys, (((1,), (1,)), ((), ())), preferred_element_type=F32
@@ -205,7 +202,7 @@
             whole = jnp.sum(weights, axis=1, keepdims=True)
             mixed = jnp.dot(weights.astype(BF16), values, preferred_element_type=F32)
             ctx[my_rows, cols] = (mixed / whole).astype(BF16)
-        cols = slice(part * heads // 2 * HEAD, (part + 1) * heads // 2 * HEAD)
+        cols = slice(part * heads // parts * HEAD, (part + 1) * heads // parts * HEAD)
         contexts.append(
             Gather(
                 block_of(ctx, cols), ctx.at[my_rows, cols], mn, m,
@@ -213,8 +210,15 @@
             )
         )
         contexts[part].start()
-    for part in range(2):
+    for part in range(parts - 1):
         contexts[part].forward()
+    for i in (2, 3, 8, 9):
+        loads[i].wait()
+    state[...] = sresid[...].astype(F32) + jnp.dot(sctx[...], sout[...], preferred_element_type=F32)
+    contexts[parts - 1].forward()
+    st[my_rows, :] = state[...].astype(BF16)
+    sq[d] = sum_to_row(state[...] * state[...])
+    gain = gain_ref[...]
     for j in range(1, n):
         exchange(sq, sq_send, sq_recv, j).start()
     student = Gather(block_of(sall), sctx, mn, m, s_send, s_recv, s_pass)
@@ -237,7 +241,7 @@
     states = Gather(block_of(st), st.at[my_rows, :], mn, m, st_send, st_recv, st_pass)
     states.start()
     loads[4].wait()
-    for part in range(2):
+    for part in range(parts):
         contexts[part].finish()
 
     def chunk(position, way):
@@ -522,7 +526,7 @@
             dma((n,)), dma((n,)), dma((n,)), dma((n,)),
             dma((mn,)), dma((mn,)),
             dma((pairs,)), dma((mn,)), dma((pairs,)),
-            dma((2, pairs)), dma((2, mn)), dma((2, pairs)),
+            dma((PARTS, pairs)), dma((PARTS, mn)), dma((PARTS, pairs)),
             dma((pairs,)), dma((mn,)), dma((pairs,)),
             dma((pairs,)), dma((mn,)), dma((pairs,)),
             dma((pairs,)), dma((mn,)), dma((pairs,)),
@@ -535,7 +539,7 @@
         teacher_query, teacher_keys, teacher_values, teacher_out, teacher_resid, distill_proj,
         student_context, student_resid, student_out, student_gain.reshape(1, width),
     )
-    steps = STEPS
+    steps = min(STEPS, features // 128)
     grad_wo, grad_gain, grad_proj = pl.pallas_call(
         finish,
         grid=(steps,),

time: 91.1 us -> 92 us (level)
    pallas_call x1, Pallas kernels: 8.69 us -> 10.2 us  [on_device(): pl.pallas_call(finish, grid=(steps,), out_shape=(jax.ShapeDtypeStruct((wi...]
where the time goes in v5:
time: 92 us; the launch traced here: 91.7 us
  Pallas kernels  91.1 us (99%)
    pallas_call x1, Pallas kernels, on_device(): pl.pallas_call(functools.partial(middle, n, mn, width, total), out_shape=...  80.9 us
    pallas_call x1, Pallas kernels, on_device(): pl.pallas_call(finish, grid=(steps,), out_shape=(jax.ShapeDtypeStruct((wi...  10.2 us

profile of v5, /device:TPU:0, one launch (start us, length us, event | category | flops | bytes accessed | tf_op | source)
XLA Modules:
  0.0 91.7 jit_solution(15829673289524609106)
XLA Ops:
  0.6 80.9 %middle.1 = (bf16[512,2048]{1,0:T(8,128)(2,1)}, bf16[512,4096]{1,0:T(8,128)(2,1)}, bf16[512,512]{1,0:T(8,128)(2,1)}, bf16[512,512]{1,0:T(8,128)(2,1)}, f32[4,16,128]{2,1,0:T(8,128)}, /*index=5*/f32[1,512]{1,0:T(1,128)}) custom-call(bf16[128,1024]{1,0:T(8,128)(2,1)} %query_hbm.1, bf16[128,1024]{1,0:T(8,128)(2,1)} %keys_hbm.1, bf16[128,1024]{1,0:T(8,128)(2,1)} %values_hbm.1, ...), custom_call_target="tpu_custom_call" | custom-call | tf_op jit(solution)/shard_map/middle/pallas_call | solution.py:484
  81.5 10.2 %finish.1 = (bf16[4096,512]{1,0:T(8,128)(2,1)}, f32[1,512]{1,0:T(1,128)}, f32[2048,512]{1,0:T(8,128)}) custom-call(bf16[512,2048]{1,0:T(8,128)(2,1)} %get-tuple-element.12.hid, bf16[512,4096]{1,0:T(8,128)(2,1)} %get-tuple-element.13.sall, bf16[512,512]{1,0:T(8,128)(2,1)} %get-tuple-element.14.err, bf16[512,512]{1,0:T(8,128)(2,1)} %get-tuple-element.15.st, ...), custom_call_target="tpu_custom_call" | custom-call | tf_op jit(solution)/shard_map/finish/pallas_call | solution.py:543

commit v6 on v5

--- a/solution.py
+++ b/solution.py
@@ -12,7 +12,7 @@
 HEAD = 128
 PIECES = 4
 PARTS = 4
-STEPS = 8
+STEPS = 4
 VMEM_BYTES = 56 * 1024 * 1024
 EPS = 1e-05
 MESH = pl.DeviceIdType.MESH
@@ -347,14 +347,19 @@
     loads[5].wait()
     project(0, False, False)
 
-    @pl.loop(1, n - 1)
+    @pl.loop(1, n // 2)
     def _(s):
         project(s, True, True)
 
+    states.forward()
+    student.forward()
+
+    @pl.loop(n // 2, n - 1)
+    def _(s):
+        project(s, True, True)
+
     project(n - 1, True, False)
     stores[2].start()
-    states.forward()
-    student.forward()
 
     exchange_wait(sq, sq_send, sq_recv)
     inverse_row = lax.rsqrt(total_of(sq) / width + EPS)
@@ -379,14 +384,28 @@
 
     error = (pred - target) * (tokens ** -0.5)
     err[my_rows, :] = error.astype(BF16)
-    errors = Gather(block_of(err), err.at[my_rows, :], mn, m, e_send, e_recv, e_pass)
-    errors.start()
+    size = rows // 2
+
+    def error_rows(part):
+        return lambda who: err.at[pl.ds(pl.multiple_of(who * rows + part * size, size), size), :]
+
+    errors = [
+        Gather(
+            error_rows(part), error_rows(part)(m), mn, m,
+            e_send.at[part], e_recv.at[part], e_pass.at[part],
+        )
+        for part in (0, 1)
+    ]
+    for part in (0, 1):
+        errors[part].start()
     inn[d] = sum_to_row(error * gain * state[...])
     for j in range(1, n):
         exchange(inn, in_send, in_recv, j).start()
 
     states.finish()
     stores[3].start()
+    for part in (0, 1):
+        errors[part].forward()
 
     exchange_wait(inn, in_send, in_recv)
     inner_row = total_of(inn)
@@ -401,9 +420,9 @@
 
     for j in range(1, mn):
         coef_copy(j).start()
-    errors.forward()
     student.finish()
-    errors.finish()
+    for part in (0, 1):
+        errors[part].finish()
     stores[4].start()
     for j in range(1, mn):
         who = (m + j) % mn
@@ -529,7 +548,7 @@
             dma((PARTS, pairs)), dma((PARTS, mn)), dma((PARTS, pairs)),
             dma((pairs,)), dma((mn,)), dma((pairs,)),
             dma((pairs,)), dma((mn,)), dma((pairs,)),
-            dma((pairs,)), dma((mn,)), dma((pairs,)),
+            dma((2, pairs)), dma((2, mn)), dma((2, pairs)),
         ],
         compiler_params=pltpu.CompilerParams(
             collective_id=0, has_side_effects=True, vmem_limit_bytes=VMEM_BYTES

time: 92 us -> 90.9 us (0.988)
  Pallas kernels: 91.1 us -> 90.1 us
    pallas_call x1, Pallas kernels: 10.2 us -> 8.69 us  [on_device(): pl.pallas_call(finish, grid=(steps,), out_shape=(jax.ShapeDtypeStruct((wi...]
where the time goes in v6:
time: 90.9 us; the launch traced here: 90.7 us
  Pallas kernels  90.1 us (99%)
    pallas_call x1, Pallas kernels, on_device(): pl.pallas_call(functools.partial(middle, n, mn, width, total), out_shape=...  81.4 us
    pallas_call x1, Pallas kernels, on_device(): pl.pallas_call(finish, grid=(steps,), out_shape=(jax.ShapeDtypeStruct((wi...  8.69 us

profile of v6, /device:TPU:0, one launch (start us, length us, event | category | flops | bytes accessed | tf_op | source)
XLA Modules:
  0.0 90.7 jit_solution(6689880262717059473)
XLA Ops:
  0.6 81.4 %middle.1 = (bf16[512,2048]{1,0:T(8,128)(2,1)}, bf16[512,4096]{1,0:T(8,128)(2,1)}, bf16[512,512]{1,0:T(8,128)(2,1)}, bf16[512,512]{1,0:T(8,128)(2,1)}, f32[4,16,128]{2,1,0:T(8,128)}, /*index=5*/f32[1,512]{1,0:T(1,128)}) custom-call(bf16[128,1024]{1,0:T(8,128)(2,1)} %query_hbm.1, bf16[128,1024]{1,0:T(8,128)(2,1)} %keys_hbm.1, bf16[128,1024]{1,0:T(8,128)(2,1)} %values_hbm.1, ...), custom_call_target="tpu_custom_call" | custom-call | tf_op jit(solution)/shard_map/middle/pallas_call | solution.py:503
  82.0 8.7 %finish.1 = (bf16[4096,512]{1,0:T(8,128)(2,1)}, f32[1,512]{1,0:T(1,128)}, f32[2048,512]{1,0:T(8,128)}) custom-call(bf16[512,2048]{1,0:T(8,128)(2,1)} %get-tuple-element.12.hid, bf16[512,4096]{1,0:T(8,128)(2,1)} %get-tuple-element.13.sall, bf16[512,512]{1,0:T(8,128)(2,1)} %get-tuple-element.14.err, bf16[512,512]{1,0:T(8,128)(2,1)} %get-tuple-element.15.st, ...), custom_call_target="tpu_custom_call" | custom-call | tf_op jit(solution)/shard_map/finish/pallas_call | solution.py:562

commit v7 on v6

--- a/solution.py
+++ b/solution.py
@@ -10,7 +10,7 @@
 HEADS = 64
 KV_HEADS = 8
 HEAD = 128
-PIECES = 4
+PIECES = 2
 PARTS = 4
 STEPS = 4
 VMEM_BYTES = 56 * 1024 * 1024

time: 90.9 us -> 98.4 us (1.083)
  Pallas kernels: 90.1 us -> 97.6 us
    pallas_call x1, Pallas kernels: 81.4 us -> 88.9 us  [on_device(): pl.pallas_call(functools.partial(middle, n, mn, width, total), out_shape=...]
where the time goes in v7:
time: 98.4 us; the launch traced here: 98.2 us
  Pallas kernels  97.6 us (99%)
    pallas_call x1, Pallas kernels, on_device(): pl.pallas_call(functools.partial(middle, n, mn, width, total), out_shape=...  88.9 us
    pallas_call x1, Pallas kernels, on_device(): pl.pallas_call(finish, grid=(steps,), out_shape=(jax.ShapeDtypeStruct((wi...  8.69 us

profile of v7, /device:TPU:0, one launch (start us, length us, event | category | flops | bytes accessed | tf_op | source)
XLA Modules:
  0.0 98.2 jit_solution(4315328996247598757)
XLA Ops:
  0.6 88.9 %middle.1 = (bf16[512,2048]{1,0:T(8,128)(2,1)}, bf16[512,4096]{1,0:T(8,128)(2,1)}, bf16[512,512]{1,0:T(8,128)(2,1)}, bf16[512,512]{1,0:T(8,128)(2,1)}, f32[4,16,128]{2,1,0:T(8,128)}, /*index=5*/f32[1,512]{1,0:T(1,128)}) custom-call(bf16[128,1024]{1,0:T(8,128)(2,1)} %query_hbm.1, bf16[128,1024]{1,0:T(8,128)(2,1)} %keys_hbm.1, bf16[128,1024]{1,0:T(8,128)(2,1)} %values_hbm.1, ...), custom_call_target="tpu_custom_call" | custom-call | tf_op jit(solution)/shard_map/middle/pallas_call | solution.py:503
  89.5 8.7 %finish.1 = (bf16[4096,512]{1,0:T(8,128)(2,1)}, f32[1,512]{1,0:T(1,128)}, f32[2048,512]{1,0:T(8,128)}) custom-call(bf16[512,2048]{1,0:T(8,128)(2,1)} %get-tuple-element.12.hid, bf16[512,4096]{1,0:T(8,128)(2,1)} %get-tuple-element.13.sall, bf16[512,512]{1,0:T(8,128)(2,1)} %get-tuple-element.14.err, bf16[512,512]{1,0:T(8,128)(2,1)} %get-tuple-element.15.st, ...), custom_call_target="tpu_custom_call" | custom-call | tf_op jit(solution)/shard_map/finish/pallas_call | solution.py:562
